TPU v7x, 32 devices: a whole 2x2x4 slice. The times are simulated.
32 devices in a mesh: dir: 2 (over core), rows: 16 (over z, y, x).
Axes of the slice: x: 2, y: 2, z: 4, core: 2. Of those that a mesh axis runs over, the one named last changes fastest.
Arguments:
- spectra: bfloat16 [16, 64, 2, 41, 128], P('rows', None, 'dir'), may hold values from -6 to 6
- mask_grad: bfloat16 [16, 64, 2, 41, 128], P('rows', None, 'dir'), may hold values from -6 to 6
- clip_starts: int32 [16, 64, 2], P('rows'), may hold values from 0 to 1, as said below
- split_weight: float32 [5248, 128], P('rows'), may hold values from -0.5 to 0.5
- split_velocity: float32 [5248, 128], P('rows'), may hold values from -0.009765625 to 0.009765625
- split_average: float32 [5248, 128], P('rows'), may hold values from -0.5 to 0.5
- lstm_weight: float32 [1536, 1024], P('rows'), may hold values from -0.3125 to 0.3125
- lstm_velocity: float32 [1536, 1024], P('rows'), may hold values from -0.009765625 to 0.009765625
- lstm_average: float32 [1536, 1024], P('rows'), may hold values from -0.3125 to 0.3125
- proj_weight: float32 [1024, 128], P('rows'), may hold values from -0.5 to 0.5
- proj_velocity: float32 [1024, 128], P('rows'), may hold values from -0.009765625 to 0.009765625
- proj_average: float32 [1024, 128], P('rows'), may hold values from -0.5 to 0.5
- up_weight: float32 [5248, 512], P('rows'), may hold values from -0.5 to 0.5
- up_velocity: float32 [5248, 512], P('rows'), may hold values from -0.009765625 to 0.009765625
- up_average: float32 [5248, 512], P('rows'), may hold values from -0.5 to 0.5
- down_weight: float32 [20992, 256], P('rows'), may hold values from -0.25 to 0.25
- down_velocity: float32 [20992, 256], P('rows'), may hold values from -0.009765625 to 0.009765625
- down_average: float32 [20992, 256], P('rows'), may hold values from -0.25 to 0.25
- gain_weight: float32 [84, 128], replicated, may hold values from 0.5 to 1.5
- gain_velocity: float32 [84, 128], replicated, may hold values from -0.009765625 to 0.009765625
- gain_average: float32 [84, 128], replicated, may hold values from 0.1 to 1.9
- bias_weight: float32 [321, 128], replicated, may hold values from -3 to 7
- bias_velocity: float32 [321, 128], replicated, may hold values from -0.009765625 to 0.009765625
- bias_average: float32 [321, 128], replicated, may hold values from -1.2 to 1.2
Outputs:
- band_mask: bfloat16 [16, 64, 2, 41, 128], P('rows', None, 'dir')
- spectra_grad: float32 [16, 64, 2, 41, 128], P('rows', None, 'dir')
- grad_norm: float32 [], replicated
- split_grad: float32 [5248, 128], P('rows')
- split_velocity_new: float32 [5248, 128], P('rows')
- split_weight_new: float32 [5248, 128], P('rows')
- split_average_new: float32 [5248, 128], P('rows')
- lstm_grad: float32 [1536, 1024], P('rows')
- lstm_velocity_new: float32 [1536, 1024], P('rows')
- lstm_weight_new: float32 [1536, 1024], P('rows')
- lstm_average_new: float32 [1536, 1024], P('rows')
- proj_grad: float32 [1024, 128], P('rows')
- proj_velocity_new: float32 [1024, 128], P('rows')
- proj_weight_new: float32 [1024, 128], P('rows')
- proj_average_new: float32 [1024, 128], P('rows')
- up_grad: float32 [5248, 512], P('rows')
- up_velocity_new: float32 [5248, 512], P('rows')
- up_weight_new: float32 [5248, 512], P('rows')
- up_average_new: float32 [5248, 512], P('rows')
- down_grad: float32 [20992, 256], P('rows')
- down_velocity_new: float32 [20992, 256], P('rows')
- down_weight_new: float32 [20992, 256], P('rows')
- down_average_new: float32 [20992, 256], P('rows')
- gain_grad: float32 [84, 128], replicated
- gain_velocity_new: float32 [84, 128], replicated
- gain_weight_new: float32 [84, 128], replicated
- gain_average_new: float32 [84, 128], replicated
- bias_grad: float32 [321, 128], replicated
- bias_velocity_new: float32 [321, 128], replicated
- bias_weight_new: float32 [321, 128], replicated
- bias_average_new: float32 [321, 128], replicated
Inputs may be any that keep to these rules, and one draw needn't show every extreme that they name: `clip_starts`: each packed sequence of 256 frames has exactly one frame flagged 1, at any of its frames; all others are 0.
All inputs are finite; a program needn't handle non-finite values.
Results may differ from a plain program's by a relative error of at most 0.018.
Values may be sent and summed in bfloat16 or wider, within the bound.
No kernel may reach another device: no remote copies, remote signals or barrier semaphores. Data moves between devices by JAX's collectives and lax.ppermute only.
A program may use at most 320 MiB of HBM per device.

v0:
```python
import functools

import jax
import jax.numpy as jnp
import numpy as np
from jax import lax
from jax.experimental import pallas as pl
from jax.experimental.pallas import tpu as pltpu
from jax.sharding import PartitionSpec as P

D = 128
H = 256
G4 = 4 * H
BANDS = 41
SUBF = 128
CHAIN = 4
SLOTS = 12
FILL = 128
ROWS_T = 16
STEPS_B = 42
VMEM = 60 << 20
PAIR = 2
HALF = (D + H) // CHAIN // 2
HALF_P = H // CHAIN // 2

EPSILON = 1e-05
MOMENTUM = 0.9
LEARN_RATE = 5.0
GAIN_RATE = 50.0
AVERAGE = 0.5
CLIP_NORM = 5.0


GAIN_TIME, GAIN_BAND, GAIN_MASK = BANDS, BANDS + 1, BANDS + 2
BIAS_LSTM = BANDS
BIAS_PROJ = BIAS_LSTM + 16 * H // D
BIAS_UP = BIAS_PROJ + 2
BIAS_DOWN = BIAS_UP + 4 * BANDS
EARLY_BIAS = BANDS
EARLY = EARLY_BIAS + BIAS_DOWN + 2 * BANDS - BIAS_PROJ - 1
EARLY_ROWS = -(-EARLY // 16) * 16
LATE_BIAS = GAIN_MASK
LATE = LATE_BIAS + BIAS_PROJ + 1
LATE_ROWS = -(-LATE // 16) * 16

BF = jnp.bfloat16
F32 = jnp.float32


def mm(a, b):
    return jnp.dot(a, b, preferred_element_type=F32)


def mm_nt(a, b):
    return lax.dot_general(a, b, (((1,), (1,)), ((), ())), preferred_element_type=F32)


def mm_tn(a, b):
    return lax.dot_general(a, b, (((0,), (0,)), ((), ())), preferred_element_type=F32)


def ln(v):
    c = v - jnp.mean(v, axis=-1, keepdims=True)
    r = lax.rsqrt(jnp.mean(c * c, axis=-1, keepdims=True) + EPSILON)
    return c * r, r


def ln_back(n, r, gain, dy):
    dg = dy * gain
    return r * (
        dg - jnp.mean(dg, axis=-1, keepdims=True) - n * jnp.mean(dg * n, axis=-1, keepdims=True)
    )


def rowsum(v):
    return jnp.sum(v, axis=0, keepdims=True)


UP_PART = 2 * D
MASK_PART = UP_PART + 4 * D
LSTM_PART = HALF * G4 // D
PROJ_PART = 2 * CHAIN * HALF_P
SHARD_PART = LSTM_PART + 2 * HALF_P
MISC_SPLIT = 2 * CHAIN * SHARD_PART
MISC_LATE = MISC_SPLIT + SLOTS * SUBF
MISC_EARLY = MISC_LATE + LATE_ROWS
MISC = MISC_EARLY + EARLY_ROWS


def shard_start(shard, rows):
    return -(-shard * BANDS // rows)


def band_blocks(rows):
    if rows == CHAIN * CHAIN:
        three = SLOTS // CHAIN
        return [
            [
                (shard_start(CHAIN * z + q, rows), three, shard_start(CHAIN * z + q + 1, rows) - shard_start(CHAIN * z + q, rows))
                for z in range(CHAIN)
            ]
            for q in range(CHAIN)
        ]
    each = BANDS // CHAIN
    return [[(each * q, SLOTS, each if q + 1 < CHAIN else BANDS - each * q)] for q in range(CHAIN)]


def band_table(rows):
    return [
        [first + i if i < filled else -1 for first, places, filled in blocks for i in range(places)]
        for blocks in band_blocks(rows)
    ]


def wide_row(rows, first, many):
    return jnp.concatenate([rows[pl.ds(first + i, 1), :] for i in range(many)], axis=1)


def forward_chunk(keep, x_ref, w_ref, bias, scale, first_row, outs, gates, hk_s, ck_s, steps, chunk, rows, unroll, hall):
    n = steps // chunk
    j = pl.program_id(0)
    first = (j * chunk, (n - 1 - j) * chunk)

    @pl.when(j == 0)
    def _():
        hk_s[...] = jnp.zeros_like(hk_s)
        ck_s[...] = jnp.zeros_like(ck_s)

    for d in range(2):
        x = x_ref[pl.ds(pl.multiple_of(first[d] * rows, chunk * rows), chunk * rows), :]
        b = wide_row(bias, first_row + d * (G4 // D), G4 // D) * scale[...]
        gates[d] = mm(x, w_ref[d, :D]) + b

    def step(t, carry):
        new = []
        for d in range(2):
            hk, ck = carry[2 * d], carry[2 * d + 1]
            tt = t if d == 0 else chunk - 1 - t
            at = first[d] + tt
            now = keep[d * steps + at]
            later = jnp.minimum(at + 1, steps - 1) if d == 0 else jnp.maximum(at - 1, 0)
            nxt = keep[d * steps + later]
            h_ref, hk_ref, cf_ref = outs[3 * d : 3 * d + 3]
            a = gates[d, pl.ds(pl.multiple_of(tt * rows, rows), rows), :] + mm(hk, w_ref[d, D:])
            ti = jnp.tanh(a[:, :H])
            tf = jnp.tanh(a[:, H : 2 * H])
            g = jnp.tanh(a[:, 2 * H : 3 * H])
            to = jnp.tanh(a[:, 3 * H :])
            i = 0.5 * ti + 0.5
            f = 0.5 * tf + 0.5
            o = 0.5 * to + 0.5
            c = f * ck + i * g
            tc = jnp.tanh(c)
            h = o * tc
            h_low = h.astype(BF)
            hk_ref[tt] = hk
            h_ref[tt] = h_low
            if hall is not None:
                hall[d, pl.ds(pl.multiple_of(at * rows, rows), rows), :] = h_low
            cf_ref[tt, :, :H] = o * (1.0 - tc * tc)
            cf_ref[tt, :, H : 2 * H] = g * (0.5 - 0.5 * ti * ti)
            cf_ref[tt, :, 2 * H : 3 * H] = ck * (0.5 - 0.5 * tf * tf)
            cf_ref[tt, :, 3 * H : 4 * H] = i * (1.0 - g * g)
            cf_ref[tt, :, 4 * H : 5 * H] = tc * (0.5 - 0.5 * to * to)
            cf_ref[tt, :, 5 * H :] = f * now
            new += [(h * nxt).astype(BF), c * nxt]
        return tuple(new)

    done = lax.fori_loop(
        0, chunk, step, (hk_s[0], ck_s[0], hk_s[1], ck_s[1]), unroll=unroll
    )
    for d in range(2):
        hk_s[d] = done[2 * d]
        ck_s[d] = done[2 * d + 1]


def backward_chunk(
    keep, x_ref, ol, w_ref, p_ref, ins, dw, dp, db, wt, pt, da, sh, rg, ch_s, cc_s, steps, chunk, rows, unroll
):
    n = steps // chunk
    j = pl.program_id(0)
    first = ((n - 1 - j) * chunk, j * chunk)
    span = chunk * rows

    @pl.when(j == 0)
    def _():
        ch_s[...] = jnp.zeros_like(ch_s)
        cc_s[...] = jnp.zeros_like(cc_s)
        rg[...] = jnp.zeros_like(rg)
        dw[...] = jnp.zeros_like(dw)
        dp[...] = jnp.zeros_like(dp)
        db[...] = jnp.zeros_like(db)
        for d in range(2):
            wt[d] = w_ref[d].T
            pt[d] = p_ref[pl.ds(d * H, H), :].T

    at_rows = [pl.ds(pl.multiple_of(first[d] * rows, span), span) for d in range(2)]
    for d in range(2):
        sh[d] = mm(ol[at_rows[d], :], pt[d]).astype(BF)

    def step(t, carry):
        new = []
        for d in range(2):
            ch, cc = carry[2 * d], carry[2 * d + 1]
            tt = chunk - 1 - t if d == 0 else t
            now = keep[d * steps + first[d] + tt]
            cf = ins[3 * d + 2]
            here = pl.ds(pl.multiple_of(tt * rows, rows), rows)
            dh = sh[d, here, :].astype(F32) + ch
            dc = cc + dh * cf[tt, :, :H]
            da_now = jnp.concatenate(
                [
                    (dc * cf[tt, :, H : 2 * H]).astype(BF),
                    (dc * cf[tt, :, 2 * H : 3 * H]).astype(BF),
                    (dc * cf[tt, :, 3 * H : 4 * H]).astype(BF),
                    (dh * cf[tt, :, 4 * H : 5 * H]).astype(BF),
                ],
                axis=-1,
            )
            da[d, here, :] = da_now
            new += [mm(da_now, wt[d, :, D:]) * now, dc * cf[tt, :, 5 * H :]]
        return tuple(new)

    done = lax.fori_loop(0, chunk, step, (ch_s[0], cc_s[0], ch_s[1], cc_s[1]), unroll=unroll)
    ones = jnp.ones((8, span), BF)
    for d in range(2):
        ch_s[d] = done[2 * d]
        cc_s[d] = done[2 * d + 1]
        here = at_rows[d]
        grad = da[d]
        rg[here, :] = rg[here, :] + mm(grad, wt[d, :, :D])
        dw[d, :D, :] = dw[d, :D, :] + mm_tn(x_ref[here, :], grad)
        dw[d, D:, :] = dw[d, D:, :] + mm_tn(ins[3 * d + 1][...].reshape(span, H), grad)
        db[d] = db[d] + mm(ones, grad)
        at_p = pl.ds(d * H, H)
        dp[at_p, :] = dp[at_p, :] + mm_tn(ins[3 * d][...].reshape(span, H), ol[here, :])


def lay_weights(side, near, far, w):
    for way in range(2):
        for q in range(CHAIN):
            for part, of in ((near, side), (far, 1 - side)):
                at = pl.multiple_of(q * 2 * HALF + of * HALF, HALF)
                w[way, pl.ds(at, HALF), :] = part[q, way, :HALF, :]


def part_totals(side, dw, dp, scale, places, proj_places):
    for way in range(2):
        for q in range(CHAIN):
            for other in range(2):
                of = 1 - side if other else side
                at = pl.multiple_of(q * 2 * HALF + of * HALF, HALF)
                part = (dw[way, pl.ds(at, HALF), :] * scale[...]).astype(BF)
                out, row = places(other, q, way)
                for c in range(G4 // D):
                    out[row + c * HALF : row + (c + 1) * HALF, :] = part[:, c * D : (c + 1) * D]
                at = pl.multiple_of(way * H + q * 2 * HALF_P + of * HALF_P, HALF_P)
                out, row = proj_places(other, q, way)
                out[row : row + HALF_P, :] = dp[pl.ds(at, HALF_P), :].astype(BF)


def bias_total(db, scale, out, first):
    for way in range(2):
        row = db[way, :1, :] * scale[...]
        for i in range(G4 // D):
            out[pl.ds(first + way * (G4 // D) + i, 1), :] = row[:, i * D : (i + 1) * D]


def band_at(meta, bands, k):
    band = bands[meta[1] * SLOTS + k]
    return jnp.maximum(band, 0), band >= 0


def time_forward_kernel(
    steps, chunk, table, keep, bands, meta, sp, sm, gain, bias, scale, near, far, p, cot,
    emb, at, br, xs, w, cot_parts, h0, hk0, cf0, h1, hk1, cf1,
    gates, hk_s, ck_s, xt, hall,
):
    n = steps // chunk
    j = pl.program_id(0)
    frames = sp.shape[2]

    @pl.when(j == 0)
    def _():
        lay_weights(meta[0], near, far, w)
        for q in range(CHAIN):
            for k in range(SLOTS):
                cot_parts[q, k] = cot[max(table[q][k], 0)]
        xt[...] = jnp.zeros_like(xt)
        for k in range(SLOTS):
            v = sp[:, k].reshape(steps, D).astype(F32)
            band = band_at(meta, bands, k)[0]
            normed = (ln(v)[0] * gain[pl.ds(band, 1), :]).astype(BF)
            e = mm(normed, sm[k]) + bias[pl.ds(band, 1), :]
            emb[:, k] = e.reshape(CHAIN, frames, D)
            xt[pl.ds(k, steps, stride=ROWS_T), :] = ln(e)[0] * gain[pl.ds(GAIN_TIME, 1), :]
        xs[...] = xt[...].astype(BF)

    forward_chunk(
        keep, xs, w, bias, scale, BIAS_LSTM, (h0, hk0, cf0, h1, hk1, cf1), gates, hk_s, ck_s, steps, chunk, ROWS_T, 16, hall
    )

    @pl.when(j == n - 1)
    def _():
        span = 512
        for s in range(0, steps * ROWS_T, span):
            here = pl.ds(s, span)
            xt[here, :] = mm(hall[0, here, :], p[:H]) + mm(hall[1, here, :], p[H:])
        for k in range(SLOTS):
            to = xt[pl.ds(k, steps, stride=ROWS_T), :] + bias[pl.ds(BIAS_PROJ, 1), :]
            a = emb[:, k].reshape(steps, D) + to
            at[:, k] = a.reshape(CHAIN, frames, D)
            br[:, k] = (ln(a)[0] * gain[pl.ds(GAIN_BAND, 1), :]).astype(BF).reshape(CHAIN, frames, D)


def band_forward_kernel(
    steps, chunk, table, keep, rows_in, cores, bias, scale, p,
    bo, xs, w, h0, hk0, cf0, h1, hk1, cf1,
    gates, hk_s, ck_s, hall,
):
    n = steps // chunk
    j = pl.program_id(0)
    frames = rows_in.shape[2]

    @pl.when(j == 0)
    def _():
        for way in range(2):
            for q in range(CHAIN):
                for core in range(2):
                    at = (2 * q + core) * HALF
                    w[way, at : at + HALF, :] = cores[q, core, way]
        for q in range(CHAIN):
            for k in range(SLOTS):
                if table[q][k] >= 0:
                    xs[pl.ds(table[q][k] * frames, frames), :] = rows_in[q, k]
        xs[pl.ds(BANDS * frames, (steps - BANDS) * frames), :] = jnp.zeros(
            ((steps - BANDS) * frames, D), BF
        )

    forward_chunk(
        keep, xs, w, bias, scale, BIAS_LSTM + 2 * G4 // D, (h0, hk0, cf0, h1, hk1, cf1), gates, hk_s, ck_s, steps, chunk, frames, 2, hall
    )

    @pl.when(j == n - 1)
    def _():
        for q in range(CHAIN):
            for k in range(SLOTS):
                here = pl.ds(max(table[q][k], 0) * frames, frames)
                bo[q, k] = (mm(hall[0, here, :], p[:H]) + mm(hall[1, here, :], p[H:])).astype(BF)


def mask_kernel(
    bands, meta, at, bo, cot, um, dm, gain, bias,
    mask, abg, abl, kept, sent, early,
):
    frames = at.shape[2]
    rows = CHAIN * frames

    both = range(PAIR)
    found = [band_at(meta, bands, pl.program_id(0) * PAIR + i) for i in both]

    @pl.when(pl.program_id(0) == 0)
    def _():
        early[...] = jnp.zeros_like(early)

    def halves(i, v, first):
        half = v.shape[1] // 2
        lower = meta[0] == 0
        near = jnp.where(lower, v[:, :half], v[:, half:]).astype(BF)
        far = jnp.where(lower, v[:, half:], v[:, :half]).astype(BF)
        many = v.shape[0]
        for c in range(half // D):
            kept[i, first + c * many : first + (c + 1) * many, :] = near[:, c * D : (c + 1) * D]
            sent[i, first + c * many : first + (c + 1) * many, :] = far[:, c * D : (c + 1) * D]

    pb = bias[pl.ds(BIAS_PROJ + 1, 1), :]
    normed = [
        ln(at[:, i].reshape(rows, D) + (bo[:, i].reshape(rows, D).astype(F32) + pb)) for i in both
    ]
    mg = [gain[pl.ds(GAIN_MASK + found[i][0], 1), :] for i in both]
    mi = [(normed[i][0] * mg[i]).astype(BF) for i in both]
    act_f = [jnp.tanh(mm(mi[i], um[i]) + wide_row(bias, BIAS_UP + 4 * found[i][0], 4)) for i in both]
    act = [v.astype(BF) for v in act_f]
    pre = [mm(act[i], dm[i]) + wide_row(bias, BIAS_DOWN + 2 * found[i][0], 2) for i in both]
    og = []
    for i in both:
        value = pre[i][:, :SUBF]
        gate = 0.5 * jnp.tanh(0.5 * pre[i][:, SUBF:]) + 0.5
        mask[:, i] = (value * gate).astype(BF).reshape(CHAIN, frames, SUBF)
        cg = cot[:, i].reshape(rows, D).astype(F32) * found[i][1].astype(F32) * gate
        og.append(jnp.concatenate([cg.astype(BF), (cg * value * (1.0 - gate)).astype(BF)], axis=-1))
    pg = [(mm_nt(og[i], dm[i]) * (1.0 - act_f[i] * act_f[i])).astype(BF) for i in both]
    dy = [mm_nt(pg[i], um[i]) for i in both]
    low = []
    for i in both:
        halves(i, mm_tn(act[i], og[i]), UP_PART)
        halves(i, mm_tn(mi[i], pg[i]), 0)
        grad = ln_back(*normed[i], mg[i], dy[i])
        abg[:, i] = grad.reshape(CHAIN, frames, D)
        low.append(grad.astype(BF))
        abl[:, i] = low[i].reshape(CHAIN, frames, D)
    sums = [
        [rowsum(v) for v in (dy[i] * normed[i][0], low[i].astype(F32), pg[i].astype(F32), og[i].astype(F32))]
        for i in both
    ]
    for i in both:
        dmg, dpb, dub, ddb = sums[i]
        band = found[i][0]

        @pl.when(found[i][1])
        def _():
            early[pl.ds(band, 1), :] = dmg
            early[pl.ds(EARLY_BIAS, 1), :] = early[pl.ds(EARLY_BIAS, 1), :] + dpb
            for c in range(4):
                row = EARLY_BIAS + BIAS_UP - BIAS_PROJ - 1 + 4 * band + c
                early[pl.ds(row, 1), :] = dub[:, c * D : (c + 1) * D]
            for c in range(2):
                row = EARLY_BIAS + BIAS_DOWN - BIAS_PROJ - 1 + 2 * band + c
                early[pl.ds(row, 1), :] = ddb[:, c * D : (c + 1) * D]


def band_backward_kernel(
    steps, chunk, table, keep, meta, scale, ol_in, xs, w, p, mask_k, mask_f, h0, hk0, cf0, h1, hk1, cf1,
    keep_w, send_w, keep_p, send_p, bias_rows, rows_out, mask_sum,
    ol, wt, pt, da, sh, rg, ch_s, cc_s, dw, dp, db,
):
    n = steps // chunk
    j = pl.program_id(0)
    frames = ol_in.shape[2]
    mask_sum[...] = mask_k[...] + mask_f[...]

    @pl.when(j == 0)
    def _():
        for q in range(CHAIN):
            for k in range(SLOTS):
                if table[q][k] >= 0:
                    ol[pl.ds(table[q][k] * frames, frames), :] = ol_in[q, k]
        ol[pl.ds(BANDS * frames, (steps - BANDS) * frames), :] = jnp.zeros(
            ((steps - BANDS) * frames, D), BF
        )

    backward_chunk(
        keep, xs, ol, w, p, (h0, hk0, cf0, h1, hk1, cf1), dw, dp, db,
        wt, pt, da, sh, rg, ch_s, cc_s, steps, chunk, frames, 2,
    )

    @pl.when(j == n - 1)
    def _():
        part_totals(
            meta[0], dw, dp, scale,
            lambda other, q, way: ((keep_w, send_w)[other], (q * 2 + way) * LSTM_PART),
            lambda other, q, way: ((keep_p, send_p)[other], (q * 2 + way) * HALF_P),
        )
        bias_total(db, scale, bias_rows, 0)
        for q in range(CHAIN):
            for k in range(SLOTS):
                if table[q][k] >= 0:
                    rows_out[q, k] = rg[pl.ds(table[q][k] * frames, frames), :].astype(BF)
                else:
                    rows_out[q, k] = jnp.zeros((frames, D), BF)


def time_backward_kernel(
    steps, chunk, keep, bands, meta, scale, bgrad, abg, at, emb, sp, sm, gain, bias_b, keep_b, send_b, early, mask, xs, w, p, h0, hk0, cf0, h1, hk1, cf1,
    keep_m, send_m, leaving,
    ol, wt, pt, da, sh, rg, ch_s, cc_s, dw, dp, db, xt, atg, late, dsm,
):
    n = steps // chunk
    j = pl.program_id(0)
    frames = bgrad.shape[2]

    @pl.when(j == 0)
    def _():
        xt[...] = jnp.zeros_like(xt)
        late[...] = jnp.zeros_like(late)
        dbg = jnp.zeros((1, D), F32)
        dpb = jnp.zeros((1, D), F32)
        for k in range(SLOTS):
            norm, r = ln(at[:, k].reshape(steps, D))
            dy = bgrad[:, k].reshape(steps, D).astype(F32)
            dbg = dbg + rowsum(dy * norm)
            a = abg[:, k].reshape(steps, D) + ln_back(norm, r, gain[pl.ds(GAIN_BAND, 1), :], dy)
            atg[k] = a
            low = a.astype(BF).astype(F32)
            dpb = dpb + rowsum(low)
            xt[pl.ds(k, steps, stride=ROWS_T), :] = low
        ol[...] = xt[...].astype(BF)
        leaving[:, :SLOTS] = mask[...]
        late[pl.ds(GAIN_BAND, 1), :] = dbg
        late[pl.ds(LATE_BIAS + BIAS_PROJ, 1), :] = dpb
        late[pl.ds(LATE_BIAS + BIAS_LSTM + 2 * G4 // D, 2 * G4 // D), :] = bias_b[...]

    backward_chunk(
        keep, xs, ol, w, p, (h0, hk0, cf0, h1, hk1, cf1), dw, dp, db,
        wt, pt, da, sh, rg, ch_s, cc_s, steps, chunk, ROWS_T, 16,
    )

    @pl.when(j == n - 1)
    def _():
        outs = (keep_m, send_m)
        part_totals(
            meta[0], dw, dp, scale,
            lambda other, q, way: (outs[other], (q * 2 + way) * SHARD_PART),
            lambda other, q, way: (outs[other], (q * 2 + way) * SHARD_PART + LSTM_PART),
        )
        bias_total(db, scale, late, LATE_BIAS + BIAS_LSTM)
        dtg = jnp.zeros((1, D), F32)
        for k in range(SLOTS):
            dy = rg[pl.ds(k, steps, stride=ROWS_T), :]
            norm, r = ln(emb[:, k].reshape(steps, D))
            dtg = dtg + rowsum(dy * norm)
            el = (atg[k] + ln_back(norm, r, gain[pl.ds(GAIN_TIME, 1), :], dy)).astype(BF)
            dsb = rowsum(el.astype(F32))
            band, filled = band_at(meta, bands, k)
            own = gain[pl.ds(band, 1), :]
            norm, r = ln(sp[:, k].reshape(steps, D).astype(F32))
            dsm[k] = mm_tn((norm * own).astype(BF), el).astype(BF)
            dy = mm_nt(el, sm[k])
            dsg = rowsum(dy * norm)

            @pl.when(filled)
            def _():
                late[pl.ds(band, 1), :] = dsg
                late[pl.ds(LATE_BIAS + band, 1), :] = dsb

            leaving[:, SLOTS + k] = ln_back(norm, r, own, dy).astype(BF).reshape(CHAIN, frames, D)
        late[pl.ds(GAIN_TIME, 1), :] = dtg
        for out, band_part in ((keep_m, keep_b), (send_m, send_b)):
            for i in range(2 * CHAIN):
                row = (i + 1) * SHARD_PART - HALF_P
                out[row : row + HALF_P, :] = band_part[i * HALF_P : (i + 1) * HALF_P, :]
            out[pl.ds(MISC_EARLY, EARLY_ROWS), :] = early[...].astype(BF)
            out[pl.ds(MISC_SPLIT, SLOTS * SUBF), :] = dsm[...].reshape(SLOTS * SUBF, D)
            out[pl.ds(MISC_LATE, LATE_ROWS), :] = late[...].astype(BF)


def assemble_kernel(table, leaving, mask, grad):
    for q in range(CHAIN):
        for k in range(SLOTS):
            if table[q][k] >= 0:
                mask[table[q][k]] = leaving[q, k]
                at = pl.ds(table[q][k], leaving.shape[2], stride=BANDS)
                grad[at, :] = leaving[q, SLOTS + k].astype(F32)


def columns_kernel(meta, own, far, up, down, over, up_s, down_s):
    many = own.shape[0]
    fill = meta[2]
    lower = meta[0] == 0
    up_s[...] = jnp.zeros_like(up_s)
    down_s[...] = jnp.zeros_like(down_s)
    for i in range(many):
        for core in range(2):
            part = jnp.where(lower == (core == 0), own[i].astype(F32), far[i].astype(F32))
            for c in range(UP_PART // D):
                at = (core * (UP_PART // D) + c) * D
                up_s[FILL + i * D : FILL + (i + 1) * D, at : at + D] = part[c * D : (c + 1) * D, :]
            down_s[4 * (FILL + i * D) : 4 * (FILL + (i + 1) * D), core * D : (core + 1) * D] = part[UP_PART:, :]
    row = 0
    for scratch, out, unit in ((up_s, up, 1), (down_s, down, 4)):
        rows, wide = out.shape
        at = pl.multiple_of((FILL - fill) * unit, 8)
        out[...] = scratch[pl.ds(at, rows), :]
        past = scratch[pl.ds(pl.multiple_of(at + rows, 8), FILL * unit), :].astype(BF)
        for c in range(wide // D):
            over[row : row + FILL * unit, :] = past[:, c * D : (c + 1) * D]
            row += FILL * unit


def totals_kernel(
    meta, up, down, before, split, split_before, near, far, _,
    lstm_t, proj_t, split_t, up_t, down_t, square, split_s,
):
    fill = meta[2]
    lower = meta[0] == 0
    for core in range(2):
        part = jnp.where(lower == (core == 0), near[...].astype(F32), far[...].astype(F32))
        for c in range(G4 // D):
            lstm_t[core * HALF : (core + 1) * HALF, c * D : (c + 1) * D] = part[c * HALF : (c + 1) * HALF, :]
        proj_t[core * HALF_P : (core + 1) * HALF_P, :] = part[LSTM_PART:, :]
    split_s[...] = jnp.zeros_like(split_s)
    split_s[FILL : FILL + split.shape[0], :] = split[...].astype(F32)
    split_t[...] = split_s[pl.ds(pl.multiple_of(FILL - fill, 8), split_t.shape[0]), :]
    up_t[...] = up[...]
    down_t[...] = down[...]
    split_t[:FILL, :] = split_t[:FILL, :] + split_before[...].astype(F32)
    row = 0
    for out, rows in ((up_t, FILL), (down_t, 4 * FILL)):
        for c in range(out.shape[1] // D):
            at = slice(c * D, (c + 1) * D)
            out[:rows, at] = out[:rows, at] + before[row : row + rows, :].astype(F32)
            row += rows
    total = jnp.zeros((1, D), F32)
    for out in (lstm_t, proj_t, split_t, up_t, down_t):
        line = rowsum(out[...] * out[...])
        for c in range(line.shape[1] // D):
            total = total + line[:, c * D : (c + 1) * D]
    square[...] = jnp.broadcast_to(jnp.sum(total, axis=-1, keepdims=True), (8, D))


def plain_call(kernel, outs, scratch, name, meta, *arrays):
    specs = [ANY if v.ndim == 4 else pl.BlockSpec(memory_space=pltpu.VMEM) for v in arrays]
    return pl.pallas_call(
        kernel,
        in_specs=([] if meta is None else [SMEM]) + specs,
        out_specs=[pl.BlockSpec(memory_space=pltpu.VMEM)] * len(outs),
        out_shape=outs,
        scratch_shapes=[pltpu.VMEM(shape, F32) for shape in scratch],
        compiler_params=pltpu.CompilerParams(vmem_limit_bytes=VMEM),
        cost_estimate=cost(3),
        name=name,
    )(*(() if meta is None else (meta,)), *arrays)


def whole(shape):
    zeros = (0,) * len(shape)
    return pl.BlockSpec(shape, lambda j: zeros)


SMEM = pl.BlockSpec(memory_space=pltpu.SMEM)
ANY = pl.BlockSpec(memory_space=pl.ANY)


def sds(shape, dtype):
    return jax.ShapeDtypeStruct(shape, dtype)


def chunk_specs(n, chunk, rows, flip):
    up = lambda j: (j, 0, 0)
    down = lambda j: (n - 1 - j, 0, 0)
    specs = []
    for way in (down, up) if flip else (up, down):
        specs += [
            pl.BlockSpec((chunk, rows, H), way),
            pl.BlockSpec((chunk, rows, H), way),
            pl.BlockSpec((chunk, rows, 6 * H), way),
        ]
    return specs


def chunk_shapes(steps, rows):
    return [
        sds((steps, rows, H), BF),
        sds((steps, rows, H), BF),
        sds((steps, rows, 6 * H), F32),
    ] * 2


def params():
    return pltpu.CompilerParams(vmem_limit_bytes=VMEM, dimension_semantics=("arbitrary",))


def cost(micros):
    return pl.CostEstimate(flops=micros * 10**9, bytes_accessed=micros * 10**6, transcendentals=0)


def time_forward(table, keep, bands, meta, sp, sm, gain, bias, scale, near, far, p, cot):
    frames = sp.shape[2]
    steps, chunk = CHAIN * frames, 32
    n = steps // chunk
    slab = (CHAIN, SLOTS, frames, D)
    return pl.pallas_call(
        functools.partial(time_forward_kernel, steps, chunk, table),
        grid=(n,),
        in_specs=[SMEM, SMEM, SMEM]
        + [whole(v.shape) for v in (sp, sm, gain, bias, scale, near, far, p, cot)],
        out_specs=[whole(slab)] * 3
        + [whole((steps * ROWS_T, D)), whole((2, D + H, G4)), whole(slab)]
        + chunk_specs(n, chunk, ROWS_T, False),
        out_shape=[sds(slab, F32), sds(slab, F32), sds(slab, BF), sds((steps * ROWS_T, D), BF), sds((2, D + H, G4), BF), sds(slab, BF)]
        + chunk_shapes(steps, ROWS_T),
        scratch_shapes=[
            pltpu.VMEM((2, chunk * ROWS_T, G4), F32),
            pltpu.VMEM((2, ROWS_T, H), BF),
            pltpu.VMEM((2, ROWS_T, H), F32),
            pltpu.VMEM((steps * ROWS_T, D), F32),
            pltpu.VMEM((2, steps * ROWS_T, H), BF),
        ],
        compiler_params=params(),
        cost_estimate=cost(66),
        name="time_forward",
    )(keep, bands, meta, sp, sm, gain, bias, scale, near, far, p, cot)


def band_forward(table, keep, rows_in, cores, bias, scale, p):
    frames = rows_in.shape[2]
    steps, chunk = STEPS_B, 14
    n = steps // chunk
    slab = (CHAIN, SLOTS, frames, D)
    return pl.pallas_call(
        functools.partial(band_forward_kernel, steps, chunk, table),
        grid=(n,),
        in_specs=[SMEM, whole(slab)] + [whole(v.shape) for v in (cores, bias, scale, p)],
        out_specs=[whole(slab), whole((steps * frames, D)), whole((2, D + H, G4))] + chunk_specs(n, chunk, frames, False),
        out_shape=[sds(slab, BF), sds((steps * frames, D), BF), sds((2, D + H, G4), BF)] + chunk_shapes(steps, frames),
        scratch_shapes=[
            pltpu.VMEM((2, chunk * frames, G4), F32),
            pltpu.VMEM((2, frames, H), BF),
            pltpu.VMEM((2, frames, H), F32),
            pltpu.VMEM((2, steps * frames, H), BF),
        ],
        compiler_params=params(),
        cost_estimate=cost(27),
        name="band_forward",
    )(keep, rows_in, cores, bias, scale, p)


def mask_stage(bands, meta, at, bo, cot, um, dm, gain, bias):
    frames = at.shape[2]
    slab = (CHAIN, SLOTS, frames, D)
    part = pl.BlockSpec((CHAIN, PAIR, frames, D), lambda k: (0, k, 0, 0))

    def band(*shape):
        return pl.BlockSpec((PAIR,) + shape, lambda k: (k, 0, 0))

    return pl.pallas_call(
        mask_kernel,
        grid=(SLOTS // PAIR,),
        in_specs=[
            SMEM, SMEM, part, part, part, band(D, 4 * D), band(4 * D, 2 * SUBF),
            whole(gain.shape), whole(bias.shape),
        ],
        out_specs=[
            part, part, part, band(MASK_PART, D), band(MASK_PART, D),
            whole((EARLY_ROWS, D)),
        ],
        out_shape=[
            sds(slab, BF), sds(slab, F32), sds(slab, BF),
            sds((SLOTS, MASK_PART, D), BF), sds((SLOTS, MASK_PART, D), BF),
            sds((EARLY_ROWS, D), F32),
        ],
        compiler_params=params(),
        cost_estimate=cost(16),
        name="mask_stage",
    )(bands, meta, at, bo, cot, um, dm, gain, bias)


def backward_scratch(steps, chunk, rows):
    span = chunk * rows
    return [
        pltpu.VMEM((steps * rows, D), BF),
        pltpu.VMEM((2, G4, D + H), BF),
        pltpu.VMEM((2, D, H), BF),
        pltpu.VMEM((2, span, G4), BF),
        pltpu.VMEM((2, span, H), BF),
        pltpu.VMEM((steps * rows, D), F32),
        pltpu.VMEM((2, rows, H), F32),
        pltpu.VMEM((2, rows, H), F32),
        pltpu.VMEM((2, D + H, G4), F32),
        pltpu.VMEM((2 * H, D), F32),
        pltpu.VMEM((2, 8, G4), F32),
    ]


def total_shapes():
    return [sds((2 * CHAIN * LSTM_PART, D), BF)] * 2 + [sds((PROJ_PART, D), BF)] * 2


def band_backward(table, keep, meta, scale, ol_in, xs, w, p, mask_k, mask_f, saved):
    frames = ol_in.shape[2]
    steps, chunk = STEPS_B, 14
    n = steps // chunk
    slab = (CHAIN, SLOTS, frames, D)
    third = pl.BlockSpec((SLOTS // n, MASK_PART, D), lambda j: (j, 0, 0))
    return pl.pallas_call(
        functools.partial(band_backward_kernel, steps, chunk, table),
        grid=(n,),
        in_specs=[SMEM, SMEM]
        + [whole(v.shape) for v in (scale, ol_in, xs, w, p)]
        + [third, third]
        + chunk_specs(n, chunk, frames, True),
        out_specs=[whole(v.shape) for v in total_shapes()] + [whole((2 * G4 // D, D)), whole(slab), third],
        out_shape=total_shapes() + [sds((2 * G4 // D, D), F32), sds(slab, BF), sds(mask_k.shape, BF)],
        scratch_shapes=backward_scratch(steps, chunk, frames),
        compiler_params=params(),
        cost_estimate=cost(32),
        name="band_backward",
    )(keep, meta, scale, ol_in, xs, w, p, mask_k, mask_f, *saved)


def time_backward(keep, bands, meta, scale, bgrad, abg, at, emb, sp, sm, gain, bias_b, keep_b, send_b, early, mask, xs, w, p, saved):
    frames = bgrad.shape[2]
    steps, chunk = CHAIN * frames, 32
    n = steps // chunk
    slab = (CHAIN, SLOTS, frames, D)
    outs = [sds((MISC, D), BF)] * 2 + [sds((CHAIN, 2 * SLOTS, frames, D), BF)]
    return pl.pallas_call(
        functools.partial(time_backward_kernel, steps, chunk),
        grid=(n,),
        in_specs=[SMEM, SMEM, SMEM]
        + [whole(v.shape) for v in (scale, bgrad, abg, at, emb, sp, sm, gain, bias_b, keep_b, send_b, early, mask, xs, w, p)]
        + chunk_specs(n, chunk, ROWS_T, True),
        out_specs=[whole(v.shape) for v in outs],
        out_shape=outs,
        scratch_shapes=backward_scratch(steps, chunk, ROWS_T)
        + [pltpu.VMEM((steps * ROWS_T, D), F32), pltpu.VMEM((SLOTS, steps, D), F32)]
        + [pltpu.VMEM((LATE_ROWS, D), F32), pltpu.VMEM((SLOTS, SUBF, D), BF)],
        compiler_params=params(),
        cost_estimate=cost(96),
        name="time_backward",
    )(keep, bands, meta, scale, bgrad, abg, at, emb, sp, sm, gain, bias_b, keep_b, send_b, early, mask, xs, w, p, *saved)


def chain_groups():
    many = lax.axis_size("rows") // CHAIN
    return [[CHAIN * g + q for q in range(CHAIN)] for g in range(many)]


def place_groups():
    many = lax.axis_size("rows") // CHAIN
    return [[CHAIN * g + q for g in range(many)] for q in range(CHAIN)]


def across(v, groups, axis=0):
    return lax.all_to_all(v, "rows", axis, axis, axis_index_groups=groups, tiled=True)


def spread(v, groups):
    return across(jnp.broadcast_to(v[None], (len(groups[0]),) + v.shape), groups)


def swap_dir(v):
    return lax.ppermute(v, "dir", [(0, 1), (1, 0)])


def ordered(side, near, far):
    return jnp.where(side == 0, jnp.stack([near, far]), jnp.stack([far, near]))


def to_bands(v, more=None):
    v = jnp.concatenate([v, v[:1]])
    parts = []
    for blocks in band_blocks(lax.axis_size("rows")):
        cuts = [v[first : first + places] for first, places, _ in blocks]
        parts.append(jnp.concatenate(cuts + ([] if more is None else [more])))
    return jnp.stack(parts)


def my_bit(bit):
    return (lax.axis_index("rows") >> bit) & 1


def swap_bit(v, bit):
    return lax.ppermute(v, "rows", [(r, r ^ (1 << bit)) for r in range(lax.axis_size("rows"))])


def double(v, bit):
    return ordered(my_bit(bit), v, swap_bit(v, bit))


def halve(v, bit, axis):
    mine = my_bit(bit)
    kept = lax.dynamic_index_in_dim(v, mine, axis, False)
    return kept + swap_bit(lax.dynamic_index_in_dim(v, 1 - mine, axis, False), bit)


def my_rows(values):
    return jnp.asarray(np.array(values, np.int32))[lax.axis_index("rows")]


def fills(rows):
    return [shard_start(s, rows) * D - s * BANDS * D // rows for s in range(rows)]


def tied(v, *others):
    for other in others:
        one = lax.slice(other, (0,) * other.ndim, (1,) * other.ndim).reshape(())
        v = jnp.where(jnp.isnan(one), jnp.zeros_like(v), v)
    return v


def rows_after(shard):
    rows = lax.axis_size("rows")
    head = FILL * (shard.shape[0] * rows // (BANDS * D))
    if not square_slice():
        return shard[:1]
    return lax.ppermute(shard[:head].astype(BF), "rows", [(r + 1, r) for r in range(rows - 1)])


def whole_bands(shard, after):
    rows = lax.axis_size("rows")
    unit = shard.shape[0] * rows // (BANDS * D)
    head = FILL * unit
    spare = jnp.zeros((head,) + shard.shape[1:], shard.dtype)
    long = jnp.concatenate([shard, after, spare])
    return lax.dynamic_slice_in_dim(long, my_rows(fills(rows)) * unit, SLOTS // CHAIN * D * unit, 0)


def past_shard(own, unit):
    rows = lax.axis_size("rows")
    fill = my_rows(fills(rows)) * unit
    head = jnp.zeros((FILL * unit,) + own.shape[1:], own.dtype)
    many = BANDS * D * unit // rows
    over = lax.dynamic_slice_in_dim(jnp.concatenate([own, head]), many - fill, FILL * unit, 0)
    return lax.ppermute(over, "rows", [(r, r + 1) for r in range(rows - 1)])


def to_shard(own, before, unit):
    rows = lax.axis_size("rows")
    fill = my_rows(fills(rows)) * unit
    many = BANDS * D * unit // rows
    head = jnp.zeros((FILL * unit,) + own.shape[1:], own.dtype)
    moved = lax.dynamic_slice_in_dim(jnp.concatenate([head, own]), FILL * unit - fill, many, 0)
    before = jnp.concatenate([before, jnp.zeros((many - FILL * unit,) + own.shape[1:], own.dtype)])
    row = lax.broadcasted_iota(jnp.int32, (many, 1), 0)
    return jnp.where(row < fill, before, moved)


def square_slice():
    return lax.axis_size("rows") == CHAIN * CHAIN


def pick_bands(wide):
    blocks = band_blocks(lax.axis_size("rows"))
    place = lax.axis_index("rows") % CHAIN
    wide = jnp.concatenate([wide, wide[:1]])
    cuts = []
    for at in range(len(blocks[0])):
        first = jnp.asarray(np.array([b[at][0] for b in blocks], np.int32))[place]
        cuts.append(lax.dynamic_slice_in_dim(wide, first, blocks[0][at][1], 0))
    return jnp.concatenate(cuts)


def place_bands(part, valid):
    blocks = band_blocks(lax.axis_size("rows"))
    place = lax.axis_index("rows") % CHAIN
    part = part * valid[:, None]
    total = jnp.zeros((BANDS + 1, part.shape[1]), F32)
    row = 0
    for at in range(len(blocks[0])):
        first = jnp.asarray(np.array([b[at][0] for b in blocks], np.int32))[place]
        cut = part[row : row + blocks[0][at][1]]
        total = lax.dynamic_update_slice_in_dim(total, cut, first, 0)
        row += blocks[0][at][1]
    return total[:BANDS]


def band_weights(shard, after, gate):
    rows = lax.axis_size("rows")
    unit = shard.shape[0] * rows // BANDS
    low = shard.astype(BF)
    if not square_slice():
        full = lax.all_gather(low, "rows", axis=0, tiled=True).reshape(BANDS, unit, -1)
        return pick_bands(full)
    own = whole_bands(low, after)
    own = tied(own, gate)
    own = lax.all_gather(own, "rows", axis=0, axis_index_groups=place_groups(), tiled=True)
    return own.reshape(SLOTS, unit, -1)


def band_sums(grads, apart):
    if not square_slice():
        return grads
    if not apart:
        return halve(halve(grads.reshape(2, 2, SLOTS // CHAIN, *grads.shape[1:]), 2, 1), 3, 0)
    return lax.psum_scatter(
        grads, "rows", scatter_dimension=0, axis_index_groups=place_groups(), tiled=True
    )


def shard_parts(own, unit):
    if not square_slice():
        return own, own
    own = own.reshape(SLOTS // CHAIN * unit, -1)
    return own, past_shard(own, unit // D)


def shard_sums(parts, unit, valid):
    own, before = parts
    if square_slice():
        return to_shard(own, before, unit // D).astype(F32)
    flat = place_bands(own.reshape(SLOTS, -1).astype(F32), valid).astype(BF)
    flat = flat.reshape(BANDS * unit, -1)
    return lax.psum_scatter(flat, "rows", scatter_dimension=0, tiled=True).astype(F32)


def both_cores(kept, sent):
    return kept + swap_dir(sent)


def mask_columns(side, own, far):
    pair = ordered(side, own, far)
    many = own.shape[0]
    up = pair[:, :, :UP_PART].reshape(2, many, UP_PART // D, D, D)
    up = jnp.transpose(up, (1, 3, 0, 2, 4)).reshape(many, D, 4 * D)
    down = jnp.transpose(pair[:, :, UP_PART:], (1, 2, 0, 3)).reshape(many, 4 * D, 2 * SUBF)
    return up, down


def sum_rows(v, bits, wire=F32):
    for bit in bits:
        v = v.astype(wire)
        v = v.astype(F32) + swap_bit(v, bit).astype(F32)
    return v


def gather_first(side, lstm_low, proj_low, split_weight, sp_parts, up_after, down_after):
    if not square_slice():
        lstm = lax.all_gather(lstm_low, "rows", axis=0, tiled=True)
        proj = lax.all_gather(proj_low, "rows", axis=0, tiled=True).reshape(2, 2 * H, D)
        cut = jnp.transpose(lstm.reshape(2, 2, CHAIN, 2, HALF, G4), (0, 3, 2, 1, 4, 5))
        sp = across(sp_parts, chain_groups())
        near = lax.dynamic_index_in_dim(cut[0], side, 0, False)
        far = lax.dynamic_index_in_dim(cut[0], 1 - side, 0, False)
        return near, far, jnp.swapaxes(cut[1], 0, 1), proj, band_weights(split_weight, None, None), sp
    flat = HALF_P * D // G4
    packed = jnp.concatenate(
        [
            lax.dynamic_slice_in_dim(lstm_low, side * HALF, HALF, 0),
            lax.dynamic_slice_in_dim(proj_low, side * HALF_P, HALF_P, 0).reshape(flat, G4),
        ]
    )
    split = whole_bands(split_weight.astype(BF), rows_after(split_weight))
    column = double(packed, 3)
    sp = across(tied(sp_parts, column), chain_groups())
    column = double(tied(column, split), 2)
    split = double(split, 3)
    time = jnp.concatenate([column[:, 0], column[:, 1, HALF:]], axis=1)
    band = column[:, 1, :HALF]
    time = tied(time, split)
    split = double(split, 2)
    time = double(time, 0)
    time = double(tied(time, split, sp, up_after, down_after), 1)
    split = jnp.swapaxes(split, 0, 1).reshape(SLOTS, SUBF, D)
    near = time.reshape(CHAIN, 2, HALF + 2 * flat, G4)
    far = swap_dir(near)
    band = ordered(side, band, swap_dir(band))
    band = spread(tied(band, near), chain_groups())
    proj = ordered(side, near[:, :, HALF:], far[:, :, HALF:]).reshape(2, CHAIN, 2, 2, flat, G4)
    proj = jnp.transpose(proj, (3, 2, 1, 0, 4, 5)).reshape(2, 2 * H, D)
    return near, far, band, proj, split, sp


def unpacked(pair):
    lead = pair.shape[:-3]
    v = jnp.swapaxes(pair.reshape(*lead, 2, G4 // D, HALF, D), -3, -2)
    return v.reshape(*lead, 2 * HALF, G4)


def traded(parts, bit):
    flat = [v.reshape(-1, D) for v in parts]
    got = swap_bit(jnp.concatenate(flat), bit)
    out, row = [], 0
    for v, rows in zip(parts, flat):
        out.append(got[row : row + rows.shape[0]].reshape(v.shape))
        row += rows.shape[0]
    return out


def cut(v, bit, axis):
    mine = my_bit(bit)
    return (
        lax.dynamic_index_in_dim(v, mine, axis, False),
        lax.dynamic_index_in_dim(v, 1 - mine, axis, False),
    )


def all_totals(side, sums, lstm_b, valid):
    v = sums[:MISC_SPLIT].reshape(CHAIN, 2, SHARD_PART, D)
    split = sums[MISC_SPLIT:MISC_LATE]
    small = sums[MISC_LATE:].astype(F32)
    if not square_slice():
        bits = range((lax.axis_size("rows") - 1).bit_length())
        band = lstm_b.reshape(CHAIN, 2, LSTM_PART, D)
        lstm = jnp.stack([v[:, :, :LSTM_PART], band])
        lstm = jnp.transpose(ordered(side, lstm, swap_dir(lstm)), (1, 3, 2, 0, 4, 5))
        lstm = unpacked(lstm).reshape(-1, G4)
        proj = v[:, :, LSTM_PART:].reshape(CHAIN, 2, 2, HALF_P, D)
        proj = jnp.transpose(ordered(side, proj, swap_dir(proj)), (3, 2, 1, 0, 4, 5)).reshape(-1, D)
        lstm, proj = (
            lax.psum_scatter(t, "rows", scatter_dimension=0, tiled=True).astype(F32) for t in (lstm, proj)
        )
        split = shard_sums((split.reshape(SLOTS, SUBF, D), None), SUBF, valid)
        return lstm, proj, split, sum_rows(small, bits, BF), small
    kept, sent = cut(v.reshape(2, 2, 2, SHARD_PART, D), 0, 1)
    got, more = traded([sent, small.astype(BF)], 0)
    v, small = kept + got, small.astype(BF).astype(F32) + more.astype(F32)
    kept, sent = cut(v, 1, 0)
    got, more = traded([sent, small.astype(BF)], 1)
    v, small = kept + got, small.astype(BF).astype(F32) + more.astype(F32)
    late = v
    time_rows = LSTM_PART + HALF_P
    band = jnp.concatenate([lstm_b.reshape(2, LSTM_PART, D), v[:, time_rows:]], axis=1)
    v = jnp.stack([v[:, :time_rows], band])
    split = split.reshape(2, 2, SLOTS // CHAIN * SUBF, D)
    for bit, axis in ((2, 1), (3, 0)):
        kept, sent = cut(v, bit, axis)
        kept_s, sent_s = cut(split, bit, axis)
        got, got_s, more = traded([sent, sent_s, small.astype(BF)], bit)
        v, split = kept + got, kept_s + got_s
        small = small.astype(BF).astype(F32) + more.astype(F32)
    return v, split, small, late


def finish_kernel(*refs):
    square, small = refs[:2]
    totals = refs[2:7]
    olds = refs[7:28]
    norm_out = refs[28]
    outs = refs[29:]
    gain_rows = [(0, LATE_BIAS, 0), (LATE_ROWS, EARLY_BIAS, LATE_BIAS)]
    bias_rows = [(LATE_BIAS, LATE - LATE_BIAS, 0), (LATE_ROWS + EARLY_BIAS, EARLY - EARLY_BIAS, LATE - LATE_BIAS)]
    line = rowsum(small[...] * small[...])
    norm = jnp.sqrt(square[:1, :1] + jnp.sum(line, axis=-1, keepdims=True))
    norm_out[...] = norm
    clip = jnp.minimum(1.0, CLIP_NORM / (norm + 1e-06))

    def put(index, at, gradient, rate):
        velocity, weight, average = olds[3 * index : 3 * index + 3]
        clipped = gradient * clip
        velocity_new = MOMENTUM * velocity[at, :] + clipped
        weight_new = weight[at, :] - rate * (clipped + MOMENTUM * velocity_new)
        results = (clipped, velocity_new, weight_new, AVERAGE * average[at, :] + (1.0 - AVERAGE) * weight_new)
        for out, value in zip(outs[4 * index : 4 * index + 4], results):
            out[at, :] = value

    for index in range(5):
        rows = totals[index].shape[0]
        put(index, slice(0, rows), totals[index][...], LEARN_RATE)
    for index, pieces in ((5, gain_rows), (6, bias_rows)):
        for first, many, at in pieces:
            put(index, slice(at, at + many), small[first : first + many, :], GAIN_RATE)


def finish(square, small, totals, olds):
    arrays = (square, small) + totals + olds
    outs = [sds((1, 1), F32)]
    for old in olds[::3]:
        outs += [sds(old.shape, F32)] * 4
    return pl.pallas_call(
        finish_kernel,
        grid=(1,),
        in_specs=[whole(v.shape) for v in arrays],
        out_specs=[whole(v.shape) for v in outs],
        out_shape=outs,
        compiler_params=params(),
        cost_estimate=cost(8),
        name="finish",
    )(*arrays)


def halved_columns():
    scale = np.full((1, G4), 0.5, np.float32)
    scale[:, 2 * H : 3 * H] = 1.0
    return jnp.asarray(scale)


def on_device(
    spectra,
    mask_grad,
    clip_starts,
    split_weight,
    split_velocity,
    split_average,
    lstm_weight,
    lstm_velocity,
    lstm_average,
    proj_weight,
    proj_velocity,
    proj_average,
    up_weight,
    up_velocity,
    up_average,
    down_weight,
    down_velocity,
    down_average,
    gain_weight,
    gain_velocity,
    gain_average,
    bias_weight,
    bias_velocity,
    bias_average,
):
    side = lax.axis_index("dir")
    row = lax.axis_index("rows")
    place = row % CHAIN
    rows = lax.axis_size("rows")
    bits = range((rows - 1).bit_length())
    frames = spectra.shape[1]
    steps = CHAIN * frames
    scale = halved_columns()
    fill = my_rows(fills(rows)) if square_slice() else place
    meta = jnp.stack([side, place, fill]).astype(jnp.int32)
    table = band_table(rows)
    valid = jnp.asarray((np.array(table) >= 0).astype(np.float32))[place]
    bands = jnp.asarray(np.array(table, np.int32).reshape(-1))

    flags = lax.dynamic_index_in_dim(clip_starts[0], side, 1, False).astype(BF)
    flag_slab = jnp.broadcast_to(flags[:, None], (frames, SUBF))
    sp_parts = to_bands(jnp.transpose(spectra[0, :, 0], (1, 0, 2)), flag_slab[None])
    up_after, down_after = rows_after(up_weight), rows_after(down_weight)
    near, far, band_w, proj, split_mat, sp = gather_first(
        side, (lstm_weight * scale).astype(BF), proj_weight.astype(BF), split_weight, sp_parts, up_after, down_after
    )
    starts = sp[:, SLOTS, :, 0].reshape(steps).astype(F32)
    keep_time = jnp.concatenate([1.0 - starts, 1.0 - starts[1:], jnp.ones((1,), F32)])
    keep_np = np.ones((2 * STEPS_B,), np.float32)
    keep_np[STEPS_B + BANDS - 1] = 0.0
    keep_band = jnp.asarray(keep_np)

    up_mat = band_weights(up_weight, up_after, near)
    down_mat = band_weights(down_weight, down_after, near)

    emb, after_time, band_rows, xs_t, w_time, cot_parts, *saved_t = time_forward(
        table, keep_time, bands, meta, sp, split_mat, gain_weight, bias_weight, scale, near, far, proj[0],
        jnp.transpose(mask_grad[0, :, 0], (1, 0, 2)),
    )
    band_out, xs_b, w_band, *saved_b = band_forward(
        table, keep_band, across(band_rows, chain_groups()), band_w, bias_weight, scale, proj[1]
    )
    mask, abg, abl, kept, sent, early = mask_stage(
        bands, meta, after_time, across(band_out, chain_groups()), across(cot_parts, chain_groups()),
        up_mat, down_mat, gain_weight, bias_weight,
    )

    ol_in = across(abl, chain_groups())
    keep_w, send_w, keep_b, send_b, bias_b, bgrad, mask_sum = band_backward(
        table, keep_band, meta, scale, ol_in, xs_b, w_band, proj[1], kept, swap_dir(sent), saved_b
    )
    bgrad = across(bgrad, chain_groups())
    lstm_sum = both_cores(tied(keep_w, bgrad), send_w)
    mask_own = band_sums(mask_sum, True)
    lstm_b = lstm_sum
    if square_slice():
        lstm_b = lax.psum_scatter(
            lstm_sum, "rows", scatter_dimension=0, axis_index_groups=chain_groups(), tiled=True
        )
    keep_m, send_m, leaving = time_backward(
        keep_time, bands, meta, scale, bgrad, abg, after_time, emb, sp, split_mat,
        gain_weight, bias_b, keep_b, send_b, early, mask, xs_t, w_time, proj[0], saved_t,
    )
    sums = both_cores(tied(keep_m, lstm_b, mask_own), send_m)
    mask_far = swap_dir(mask_own)
    if square_slice():
        units = BANDS * D // rows
        up_own, down_own, over = plain_call(
            columns_kernel,
            [
                sds((units, 4 * D), F32), sds((4 * units, 2 * SUBF), F32),
                sds((FILL * 4 + 4 * FILL * 2, D), BF),
            ],
            [(5 * D, 4 * D), (20 * D, 2 * SUBF)], "mask_columns", meta, mask_own, mask_far,
        )
        before = lax.ppermute(over, "rows", [(r, r + 1) for r in range(rows - 1)])
        v, split, small, _ = all_totals(side, sums, lstm_b, valid)
        leaving = across(leaving, chain_groups())
        split_before = past_shard(split, 1)
        lstm_total, proj_total, split_total, up_total, down_total, square = plain_call(
            totals_kernel,
            [
                sds(lstm_weight.shape, F32), sds(proj_weight.shape, F32), sds(split_weight.shape, F32),
                sds(up_weight.shape, F32), sds(down_weight.shape, F32), sds((8, D), F32),
            ],
            [(5 * D, D)], "totals", meta, up_own, down_own, before, split, split_before,
            v, swap_dir(v), leaving,
        )
    else:
        up_own, down_own = mask_columns(side, mask_own, mask_far)
        lstm_total, proj_total, split_total, small, _ = all_totals(side, sums, lstm_b, valid)
        leaving = across(leaving, chain_groups())
        up_total = shard_sums(shard_parts(up_own, D), D, valid)
        down_total = shard_sums(shard_parts(down_own, 4 * D), 4 * D, valid)
        parts = (split_total, lstm_total, proj_total, up_total, down_total)
        square = jnp.full((8, D), sum(jnp.sum(v * v) for v in parts), F32)
    band_mask, spectra_grad = pl.pallas_call(
        functools.partial(assemble_kernel, table),
        grid=(1,),
        in_specs=[whole(leaving.shape)],
        out_specs=[whole((BANDS, frames, D)), whole((frames * BANDS, D))],
        out_shape=[sds((BANDS, frames, D), BF), sds((frames * BANDS, D), F32)],
        compiler_params=params(),
        cost_estimate=cost(3),
        name="assemble",
    )(leaving)
    band_mask = jnp.transpose(band_mask, (1, 0, 2))[None, :, None]
    spectra_grad = spectra_grad.reshape(1, frames, 1, BANDS, D)
    square = sum_rows(square, bits)
    norm, *results = finish(
        square,
        small,
        (split_total, lstm_total, proj_total, up_total, down_total),
        (
            split_velocity, split_weight, split_average, lstm_velocity, lstm_weight, lstm_average,
            proj_velocity, proj_weight, proj_average, up_velocity, up_weight, up_average,
            down_velocity, down_weight, down_average, gain_velocity, gain_weight, gain_average,
            bias_velocity, bias_weight, bias_average,
        ),
    )
    return (band_mask, spectra_grad, norm.reshape(())) + tuple(results)


def solution(mesh):
    per_row = P("rows", None)
    row_major = P("rows", None, "dir", None, None)
    return jax.shard_map(
        on_device,
        mesh=mesh,
        in_specs=(row_major, row_major, P("rows", None, None)) + (per_row,) * 15 + (P(),) * 6,
        out_specs=(row_major, row_major, P()) + (per_row,) * 20 + (P(),) * 8,
        check_vma=False,
    )
```

profile of v0, /device:TPU:0, one launch (start us, length us, event | category | flops | bytes accessed | tf_op | source)
XLA Modules:
  0.0 502.3 jit_solution(17714331393214838543)
XLA Ops:
  11.2 7.1 %collective-permute-start = (bf16[52,1024]{1,0:T(8,128)(2,1)S(1)}, bf16[52,1024]{1,0:T(8,128)(2,1)S(1)}, u32[]{:S(2)}, u32[]{:S(2)}) collective-permute-start(bf16[52,1024]{1,0:T(8,128)(2,1)S(1)} %get-tuple-element.277), channel_id=1, source_target_pairs={{0,8},{1,9},{2,10},{3,11},{4,12},{5,13},{6,14},{7,15},{8,0},{9,1},... | collective-permute-start | bytes 319496 | tf_op jit(solution)/shard_map/ppermute | solution.py:844
  26.9 5.8 %collective-permute-start.2 = (bf16[384,128]{1,0:T(8,128)(2,1)S(1)}, bf16[384,128]{1,0:T(8,128)(2,1)S(1)}, u32[]{:S(2)}, u32[]{:S(2)}) collective-permute-start(bf16[384,128]{1,0:T(8,128)(2,1)S(1)} %fusion.23), channel_id=1, source_target_pairs={{0,8},{1,9},{2,10},{3,11},{4,12},{5,13},{6,14},{7,15},{8,0},{9,1},... | collective-permute-start | bytes 294920 | tf_op jit(solution)/shard_map/ppermute | solution.py:844
  37.5 3.5 all-to-all-start
  60.5 7.5 %collective-permute-done.8 = bf16[2,2,56,1024]{3,2,1,0:T(8,128)(2,1)} collective-permute-done((bf16[2,2,56,1024]{3,2,1,0:T(8,128)(2,1)}, bf16[2,2,56,1024]{3,2,1,0:T(8,128)(2,1)}, u32[]{:S(2)}, u32[]{:S(2)}) %collective-permute-start.8) | collective-permute-done | bytes 458784 | tf_op jit(solution)/shard_map/ppermute | solution.py:844
  79.1 3.7 all-to-all-start.2
  87.6 64.9 %time_forward.1 = (f32[4,12,64,128]{3,2,1,0:T(8,128)}, f32[4,12,64,128]{3,2,1,0:T(8,128)}, bf16[4,12,64,128]{3,2,1,0:T(8,128)(2,1)}, bf16[4096,128]{1,0:T(8,128)...) custom-call(f32[512]{0:T(512)} %pad_maximum_fusion.8.keep, ...), custom_call_target="tpu_custom_call" | custom-call | flops 65999998976 | bytes 66000000 | tf_op jit(solution)/shard_map/time_forward/pallas_call | solution.py:662
  152.6 4.2 all-to-all-start.1
  157.5 9.8 %all-to-all-done.1.rows_in = bf16[4,12,64,128]{3,2,1,0:T(8,128)(2,1)S(1)} async-done(((bf16[4,12,64,128]{3,2,1,0:T(8,128)(2,1)}), bf16[4,12,64,128]{3,2,1,0:T(8,128)(2,1)S(1)}, u32[]{:S(2)}, u32[]{:S(2)}) %all-to-all-start.1) | async-done | bytes 786464 | tf_op jit(solution)/shard_map/all_to_all | solution.py:815
  168.2 3.5 all-to-all-start.4
  171.8 25.5 %band_forward.1 = (bf16[4,12,64,128]{3,2,1,0:T(8,128)(2,1)}, bf16[2688,128]{1,0:T(8,128)(2,1)}, bf16[2,384,1024]{2,1,0:T(8,128)(2,1)}, bf16[42,64,256]{2,1,0:T(8...) custom-call(f32[84]{0:T(128)} %constant.125.clone.keep, ...), custom_call_target="tpu_custom_call" | custom-call | flops 27000000512 | bytes 27000000 | tf_op jit(solution)/shard_map/band_forward/pallas_call | solution.py:690
  197.3 15.3 %all_to_all.40.bo = bf16[4,12,64,128]{3,2,1,0:T(8,128)(2,1)} all-to-all(bf16[4,12,64,128]{3,2,1,0:T(8,128)(2,1)} %get-tuple-element.110), channel_id=1, replica_groups={{0,1,2,3},{4,5,6,7},{8,9,10,11},{12,13,14,15},{16,17,18,19},{20,21,22,2..., dimensions={0} | all-to-all | bytes 1572864 | tf_op jit(solution)/shard_map/all_to_all | solution.py:815
  212.7 12.0 %mask_stage.1 = (bf16[4,12,64,128]{3,2,1,0:T(8,128)(2,1)}, f32[4,12,64,128]{3,2,1,0:T(8,128)}, bf16[4,12,64,128]{3,2,1,0:T(8,128)(2,1)}, bf16[12,768,128]{2,1,0:...) custom-call(s32[48]{0:T(128)} %constant.124.clone.bands, s32[3]{0:T(128)} %pad_add_fusion.meta, ...), custom_call_target="tpu_custom_call" | custom-call | flops 16000000000 | bytes 16000000 | tf_op jit(solution)/shard_map/mask_stage/pallas_call | solution.py:716
  224.8 16.5 %all_to_all.41.ol_in = bf16[4,12,64,128]{3,2,1,0:T(8,128)(2,1)} all-to-all(bf16[4,12,64,128]{3,2,1,0:T(8,128)(2,1)} %get-tuple-element.112), channel_id=1, replica_groups={{0,1,2,3},{4,5,6,7},{8,9,10,11},{12,13,14,15},{16,17,18,19},{20,21,22,2..., dimensions={0} | all-to-all | bytes 1572864 | tf_op jit(solution)/shard_map/all_to_all | solution.py:815
  242.8 34.9 %band_backward.1 = (bf16[3072,128]{1,0:T(8,128)(2,1)}, bf16[3072,128]{1,0:T(8,128)(2,1)}, bf16[256,128]{1,0:T(8,128)(2,1)}, bf16[256,128]{1,0:T(8,128)(2,1)}, f3...) custom-call(f32[84]{0:T(128)} %constant.125.clone.keep, s32[3]{0:T(128)} %pad_add_fusion.meta, ...), custom_call_target="tpu_custom_call" | custom-call | flops 32000000000 | bytes 32000000 | tf_op jit(solution)/shard_map/band_backward/pallas_call | solution.py:765
  277.7 15.7 %all_to_all.42.bgrad = bf16[4,12,64,128]{3,2,1,0:T(8,128)(2,1)S(1)} all-to-all(bf16[4,12,64,128]{3,2,1,0:T(8,128)(2,1)} %get-tuple-element.123), channel_id=1, replica_groups={{0,1,2,3},{4,5,6,7},{8,9,10,11},{12,13,14,15},{16,17,18,19},{20,21,22,2..., dimensions={0} | all-to-all | bytes 1572864 | tf_op jit(solution)/shard_map/all_to_all | solution.py:815
  296.9 96.4 %time_backward.1 = (bf16[5536,128]{1,0:T(8,128)(2,1)}, bf16[5536,128]{1,0:T(8,128)(2,1)}, bf16[4,24,64,128]{3,2,1,0:T(8,128)(2,1)}) custom-call(f32[512]{0:T(512)} %pad_maximum_fusion.8.keep, s32[48]{0:T(128)} %constant.124.clone.bands, s32[3]{0:T(128)} %pad_add_fusion.meta, f32[1,1024]{1,0:T(1,128)} %constant.122.clone.scale, ...), custom_call_target="tpu_custom_call" | custom-call | flops 96000000000 | bytes 96000000 | tf_op jit(solution)/shard_map/time_backward/pallas_call | solution.py:787
  401.8 14.5 %collective-permute-done.16 = bf16[2208,128]{1,0:T(8,128)(2,1)S(1)} collective-permute-done((bf16[2208,128]{1,0:T(8,128)(2,1)}, bf16[2208,128]{1,0:T(8,128)(2,1)S(1)}, u32[]{:S(2)}, u32[]{:S(2)}) %collective-permute-start.16) | collective-permute-done | bytes 565280 | tf_op jit(solution)/shard_map/ppermute | solution.py:844
  417.6 8.4 %collective-permute-done.17 = bf16[1312,128]{1,0:T(8,128)(2,1)S(1)} collective-permute-done((bf16[1312,128]{1,0:T(8,128)(2,1)S(1)}, bf16[1312,128]{1,0:T(8,128)(2,1)S(1)}, u32[]{:S(2)}, u32[]{:S(2)}) %collective-permute-start.17) | collective-permute-done | bytes 335904 | tf_op jit(solution)/shard_map/ppermute | solution.py:844
  429.6 3.6 all-to-all-start.7
  433.3 7.5 %collective-permute-done.18 = bf16[2016,128]{1,0:T(8,128)(2,1)} collective-permute-done((bf16[2016,128]{1,0:T(8,128)(2,1)}, bf16[2016,128]{1,0:T(8,128)(2,1)}, u32[]{:S(2)}, u32[]{:S(2)}) %collective-permute-start.18) | collective-permute-done | bytes 516128 | tf_op jit(solution)/shard_map/ppermute | solution.py:844
  452.6 5.9 %collective-permute-done.19 = bf16[1216,128]{1,0:T(8,128)(2,1)S(1)} collective-permute-done((bf16[1216,128]{1,0:T(8,128)(2,1)S(1)}, bf16[1216,128]{1,0:T(8,128)(2,1)S(1)}, u32[]{:S(2)}, u32[]{:S(2)}) %collective-permute-start.19) | collective-permute-done | bytes 311328 | tf_op jit(solution)/shard_map/ppermute | solution.py:844
  463.8 3.3 totals.1
  480.1 4.7 collective-permute-start.25
  487.0 8.6 %finish.1 = (f32[1,1]{1,0:T(1,128)}, f32[328,128]{1,0:T(8,128)}, f32[328,128]{1,0:T(8,128)}, f32[328,128]{1,0:T(8,128)}, f32[328,128]{1,0:T(8,128)}, /*index=5*/...) custom-call(f32[8,128]{1,0:T(8,128)} %add.160.refs_0_, ...), custom_call_target="tpu_custom_call" | custom-call | flops 8000000000 | bytes 8000000 | tf_op jit(solution)/shard_map/finish/pallas_call | solution.py:1130
  (204 shorter events, 86.2 us)
Async XLA Ops:
  8.1 17.9 %collective-permute-start.1 = (bf16[128,128]{1,0:T(8,128)(2,1)S(1)}, bf16[128,128]{1,0:T(8,128)(2,1)S(1)}, u32[]{:S(2)}, u32[]{:S(2)}) collective-permute-start(bf16[128,128]{1,0:T(8,128)(2,1)S(1)} %slice.247), channel_id=1, source_target_pairs={{1,0},{2,1},{3,2},{4,3},{5,4},{6,5},{7,6},{8,7},{9,8},{10,9},{11,1... | collective-permute-start | bytes 98312 | tf_op jit(solution)/shard_map/ppermute | solution.py:877
  11.2 22.8 %collective-permute-start = (bf16[52,1024]{1,0:T(8,128)(2,1)S(1)}, bf16[52,1024]{1,0:T(8,128)(2,1)S(1)}, u32[]{:S(2)}, u32[]{:S(2)}) collective-permute-start(bf16[52,1024]{1,0:T(8,128)(2,1)S(1)} %get-tuple-element.277), channel_id=1, source_target_pairs={{0,8},{1,9},{2,10},{3,11},{4,12},{5,13},{6,14},{7,15},{8,0},{9,1},... | collective-permute-start | bytes 319496 | tf_op jit(solution)/shard_map/ppermute | solution.py:844
  20.4 26.5 %collective-permute-start.4 = (bf16[512,256]{1,0:T(8,128)(2,1)}, bf16[512,256]{1,0:T(8,128)(2,1)}, u32[]{:S(2)}, u32[]{:S(2)}) collective-permute-start(bf16[512,256]{1,0:T(8,128)(2,1)} %slice.248), channel_id=1, source_target_pairs={{1,0},{2,1},{3,2},{4,3},{5,4},{6,5},{7,6},{8,7},{9,8},{10,9},{11,1... | collective-permute-start | bytes 786440 | tf_op jit(solution)/shard_map/ppermute | solution.py:877
  21.8 23.3 %collective-permute-start.5 = (bf16[128,512]{1,0:T(8,128)(2,1)S(1)}, bf16[128,512]{1,0:T(8,128)(2,1)S(1)}, u32[]{:S(2)}, u32[]{:S(2)}) collective-permute-start(bf16[128,512]{1,0:T(8,128)(2,1)S(1)} %slice.250), channel_id=1, source_target_pairs={{1,0},{2,1},{3,2},{4,3},{5,4},{6,5},{7,6},{8,7},{9,8},{10,9},{11,1... | collective-permute-start | bytes 393224 | tf_op jit(solution)/shard_map/ppermute | solution.py:877
  26.9 14.3 %collective-permute-start.2 = (bf16[384,128]{1,0:T(8,128)(2,1)S(1)}, bf16[384,128]{1,0:T(8,128)(2,1)S(1)}, u32[]{:S(2)}, u32[]{:S(2)}) collective-permute-start(bf16[384,128]{1,0:T(8,128)(2,1)S(1)} %fusion.23), channel_id=1, source_target_pairs={{0,8},{1,9},{2,10},{3,11},{4,12},{5,13},{6,14},{7,15},{8,0},{9,1},... | collective-permute-start | bytes 294920 | tf_op jit(solution)/shard_map/ppermute | solution.py:844
  34.7 14.7 %collective-permute-start.6 = (bf16[2,52,1024]{2,1,0:T(8,128)(2,1)}, bf16[2,52,1024]{2,1,0:T(8,128)(2,1)}, u32[]{:S(2)}, u32[]{:S(2)}) collective-permute-start(bf16[2,52,1024]{2,1,0:T(8,128)(2,1)} %get-tuple-element.247), channel_id=1, source_target_pairs={{0,4},{1,5},{2,6},{3,7},{4,0},{5,1},{6,2},{7,3},{8,12},{9,13},{10,... | collective-permute-start | bytes 638984 | tf_op jit(solution)/shard_map/ppermute | solution.py:844
  37.5 17.7 %all-to-all-start = ((bf16[4,13,64,128]{3,2,1,0:T(8,128)(2,1)}), bf16[4,13,64,128]{3,2,1,0:T(8,128)(2,1)S(1)}, u32[]{:S(2)}, u32[]{:S(2)}) async-start(bf16[4,13,64,128]{3,2,1,0:T(8,128)(2,1)} %maximum_select_fusion.1), calls=%async_computation | async-start | bytes 1703936 | tf_op jit(solution)/shard_map/all_to_all | solution.py:815
  41.0 171.6 %all-gather.3.cloned.1.call-start = ((), (), s32[]{:S(2)}) async-start(), calls=%async_computation.10 | async-start | bytes 1966080 | tf_op jit(solution)/shard_map/all_gather | solution.py:947
  41.7 11.6 %collective-permute-start.3 = (bf16[2,384,128]{2,1,0:T(8,128)(2,1)S(1)}, bf16[2,384,128]{2,1,0:T(8,128)(2,1)S(1)}, u32[]{:S(2)}, u32[]{:S(2)}) collective-permute-start(bf16[2,384,128]{2,1,0:T(8,128)(2,1)S(1)} %maximum_select_fusion.12), channel_id=1, source_target_pairs={{0,4},{1,5},{2,6},{3,7},{4,0},{5,1},{6,2},{7,3},{8,12},{9,13},{10,... | collective-permute-start | bytes 589832 | tf_op jit(solution)/shard_map/ppermute | solution.py:844
  58.5 9.6 %collective-permute-start.8 = (bf16[2,2,56,1024]{3,2,1,0:T(8,128)(2,1)}, bf16[2,2,56,1024]{3,2,1,0:T(8,128)(2,1)}, u32[]{:S(2)}, u32[]{:S(2)}) collective-permute-start(bf16[2,2,56,1024]{3,2,1,0:T(8,128)(2,1)} %fusion.10), channel_id=1, source_target_pairs={{0,2},{1,3},{2,0},{3,1},{4,6},{5,7},{6,4},{7,5},{8,10},{9,11},{10,... | collective-permute-start | bytes 1376264 | tf_op jit(solution)/shard_map/ppermute | solution.py:844
  79.1 73.5 %all-to-all-start.2 = ((bf16[4,2,2,48,1024]{4,3,2,1,0:T(8,128)(2,1)}), bf16[4,2,2,48,1024]{4,3,2,1,0:T(8,128)(2,1)S(1)}, u32[]{:S(2)}, u32[]{:S(2)}) async-start(bf16[4,2,2,48,1024]{4,3,2,1,0:T(8,128)(2,1)} %broadcast_in_dim.47), calls=%async_computation.2 | async-start | bytes 3145728 | tf_op jit(solution)/shard_map/all_to_all | solution.py:815
  82.8 129.9 %all-gather.5.cloned.1.call-start = ((), (), s32[]{:S(2)}) async-start(), calls=%async_computation.11 | async-start | bytes 3932160 | tf_op jit(solution)/shard_map/all_gather | solution.py:947
  152.6 14.8 %all-to-all-start.1 = ((bf16[4,12,64,128]{3,2,1,0:T(8,128)(2,1)}), bf16[4,12,64,128]{3,2,1,0:T(8,128)(2,1)S(1)}, u32[]{:S(2)}, u32[]{:S(2)}) async-start(bf16[4,12,64,128]{3,2,1,0:T(8,128)(2,1)} %get-tuple-element.109), calls=%async_computation.1 | async-start | bytes 1572864 | tf_op jit(solution)/shard_map/all_to_all | solution.py:815
  168.2 29.1 %all-to-all-start.4 = ((bf16[4,12,64,128]{3,2,1,0:T(8,128)(2,1)}), bf16[4,12,64,128]{3,2,1,0:T(8,128)(2,1)S(1)}, u32[]{:S(2)}, u32[]{:S(2)}) async-start(bf16[4,12,64,128]{3,2,1,0:T(8,128)(2,1)} %get-tuple-element.111), calls=%async_computation.4 | async-start | bytes 1572864 | tf_op jit(solution)/shard_map/all_to_all | solution.py:815
  171.8 221.7 %reduce-scatter.5.cloned.1.call-start = ((), (), s32[]{:S(2)}) async-start(), calls=%async_computation.13 | async-start | bytes 983040 | tf_op jit(solution)/shard_map/reduce_scatter | solution.py:1225
  224.7 16.6 %collective-permute-start.11 = (bf16[12,768,128]{2,1,0:T(8,128)(2,1)}, bf16[12,768,128]{2,1,0:T(8,128)(2,1)S(1)}, u32[]{:S(2)}, u32[]{:S(2)}) collective-permute-start(bf16[12,768,128]{2,1,0:T(8,128)(2,1)} %get-tuple-element.116), channel_id=1, source_target_pairs={{0,16},{16,0},{1,17},{17,1},{2,18},{18,2},{3,19},{19,3},{4,20},{20... | collective-permute-start | bytes 7077896 | tf_op jit(solution)/shard_map/ppermute | solution.py:823
  277.6 17.7 %collective-permute-start.14 = (bf16[3072,128]{1,0:T(8,128)(2,1)}, bf16[3072,128]{1,0:T(8,128)(2,1)S(1)}, u32[]{:S(2)}, u32[]{:S(2)}) collective-permute-start(bf16[3072,128]{1,0:T(8,128)(2,1)} %get-tuple-element.147), channel_id=1, source_target_pairs={{0,16},{16,0},{1,17},{17,1},{2,18},{18,2},{3,19},{19,3},{4,20},{20... | collective-permute-start | bytes 2359304 | tf_op jit(solution)/shard_map/ppermute | solution.py:823
  296.3 99.6 %reduce-scatter.3.cloned.1.call-start = ((), (), s32[]{:S(2)}) async-start(), calls=%async_computation.12 | async-start | bytes 2949120 | tf_op jit(solution)/shard_map/reduce_scatter | solution.py:956
  400.9 15.4 %collective-permute-start.16 = (bf16[2208,128]{1,0:T(8,128)(2,1)}, bf16[2208,128]{1,0:T(8,128)(2,1)S(1)}, u32[]{:S(2)}, u32[]{:S(2)}) collective-permute-start(bf16[2208,128]{1,0:T(8,128)(2,1)} %pad_maximum_fusion), channel_id=1, source_target_pairs={{0,1},{1,0},{2,3},{3,2},{4,5},{5,4},{6,7},{7,6},{8,9},{9,8},{10,11... | collective-permute-start | bytes 1695752 | tf_op jit(solution)/shard_map/ppermute | solution.py:844
  428.0 12.8 %collective-permute-start.18 = (bf16[2016,128]{1,0:T(8,128)(2,1)}, bf16[2016,128]{1,0:T(8,128)(2,1)}, u32[]{:S(2)}, u32[]{:S(2)}) collective-permute-start(bf16[2016,128]{1,0:T(8,128)(2,1)} %pad_maximum_fusion.1), channel_id=1, source_target_pairs={{0,4},{1,5},{2,6},{3,7},{4,0},{5,1},{6,2},{7,3},{8,12},{9,13},{10,... | collective-permute-start | bytes 1548296 | tf_op jit(solution)/shard_map/ppermute | solution.py:844
  429.6 31.9 %all-to-all-start.7 = ((bf16[4,24,64,128]{3,2,1,0:T(8,128)(2,1)}), bf16[4,24,64,128]{3,2,1,0:T(8,128)(2,1)S(1)}, u32[]{:S(2)}, u32[]{:S(2)}) async-start(bf16[4,24,64,128]{3,2,1,0:T(8,128)(2,1)} %get-tuple-element.139), calls=%async_computation.7 | async-start | bytes 3145728 | tf_op jit(solution)/shard_map/all_to_all | solution.py:815
  433.2 13.5 %collective-permute-start.12 = (bf16[3,768,128]{2,1,0:T(8,128)(2,1)}, bf16[3,768,128]{2,1,0:T(8,128)(2,1)}, u32[]{:S(2)}, u32[]{:S(2)}) collective-permute-start(bf16[3,768,128]{2,1,0:T(8,128)(2,1)} %reduce-scatter.3.cloned.1.call-done.own), channel_id=1, source_target_pairs={{0,16},{16,0},{1,17},{17,1},{2,18},{18,2},{3,19},{19,3},{4,20},{20... | collective-permute-start | bytes 1769480 | tf_op jit(solution)/shard_map/ppermute | solution.py:823
  443.7 14.8 %collective-permute-start.19 = (bf16[1216,128]{1,0:T(8,128)(2,1)S(1)}, bf16[1216,128]{1,0:T(8,128)(2,1)S(1)}, u32[]{:S(2)}, u32[]{:S(2)}) collective-permute-start(bf16[1216,128]{1,0:T(8,128)(2,1)S(1)} %pad_maximum_fusion.3), channel_id=1, source_target_pairs={{0,8},{1,9},{2,10},{3,11},{4,12},{5,13},{6,14},{7,15},{8,0},{9,1},... | collective-permute-start | bytes 933896 | tf_op jit(solution)/shard_map/ppermute | solution.py:844
  449.8 11.8 %collective-permute-start.13 = (bf16[1536,128]{1,0:T(8,128)(2,1)}, bf16[1536,128]{1,0:T(8,128)(2,1)S(1)}, u32[]{:S(2)}, u32[]{:S(2)}) collective-permute-start(bf16[1536,128]{1,0:T(8,128)(2,1)} %get-tuple-element.145), channel_id=1, source_target_pairs={{0,1},{1,2},{2,3},{3,4},{4,5},{5,6},{6,7},{7,8},{8,9},{9,10},{10,1... | collective-permute-start | bytes 1179656 | tf_op jit(solution)/shard_map/ppermute | solution.py:1244
  (29 other events, 181.1 us)
Sparse Core Ops, SparseCore 0:
  72.4 36.1 all-gather.2
  110.2 62.3 all-gather.4
  296.4 23.9 reduce-scatter.4
  322.6 48.0 reduce-scatter.2
where the time goes:
time: 508 us; the launch traced here: 502 us
  Pallas kernels  252 us (50%)
  starting transfers between devices  63.8 us (13%)
  waiting for transfers between devices  60.7 us (12%)
  blocking collectives  47.6 us (9%)
  between operations  33.1 us (7%)
  other arithmetic  25.2 us (5%)
  local copies, waits for them, and re-layouts  20.2 us (4%)
    pallas_call x1, Pallas kernels, time_backward(): pl.pallas_call(functools.partial(time_backward_kernel, steps, chunk), gri...  96.4 us
    pallas_call x1, Pallas kernels, time_forward(): pl.pallas_call(functools.partial(time_forward_kernel, steps, chunk, table...  64.9 us
    ppermute x14, waiting for transfers between devices, swap_bit(): lax.ppermute(v, 'rows', [(r, r ^ 1 << bit) for r in range(lax.axis_size('...  48.7 us
    all_to_all x3, blocking collectives, across(): lax.all_to_all(v, 'rows', axis, axis, axis_index_groups=groups, tiled=True)  47.6 us
    pallas_call x1, Pallas kernels, band_backward(): pl.pallas_call(functools.partial(band_backward_kernel, steps, chunk, tabl...  34.9 us
    ppermute x14, starting transfers between devices, swap_bit(): lax.ppermute(v, 'rows', [(r, r ^ 1 << bit) for r in range(lax.axis_size('...  34.6 us
    pallas_call x1, Pallas kernels, band_forward(): pl.pallas_call(functools.partial(band_forward_kernel, steps, chunk, table...  25.5 us
    all_to_all x5, starting transfers between devices, across(): lax.all_to_all(v, 'rows', axis, axis, axis_index_groups=groups, tiled=True)  18.5 us
  transfers between devices with their start and end apart: 35, of which 12 were waited for; matrix products, arithmetic and copies ran while one was open for 6% of the time, Pallas kernels for 38%

commit v1 on v0

--- a/solution.py
+++ b/solution.py
@@ -19,7 +19,7 @@
 ROWS_T = 16
 STEPS_B = 42
 VMEM = 60 << 20
-PAIR = 2
+PAIR = 3
 HALF = (D + H) // CHAIN // 2
 HALF_P = H // CHAIN // 2
 
@@ -297,7 +297,7 @@
         xs[...] = xt[...].astype(BF)
 
     forward_chunk(
-        keep, xs, w, bias, scale, BIAS_LSTM, (h0, hk0, cf0, h1, hk1, cf1), gates, hk_s, ck_s, steps, chunk, ROWS_T, 16, hall
+        keep, xs, w, bias, scale, BIAS_LSTM, (h0, hk0, cf0, h1, hk1, cf1), gates, hk_s, ck_s, steps, chunk, ROWS_T, 32, hall
     )
 
     @pl.when(j == n - 1)
@@ -338,7 +338,7 @@
         )
 
     forward_chunk(
-        keep, xs, w, bias, scale, BIAS_LSTM + 2 * G4 // D, (h0, hk0, cf0, h1, hk1, cf1), gates, hk_s, ck_s, steps, chunk, frames, 2, hall
+        keep, xs, w, bias, scale, BIAS_LSTM + 2 * G4 // D, (h0, hk0, cf0, h1, hk1, cf1), gates, hk_s, ck_s, steps, chunk, frames, 7, hall
     )
 
     @pl.when(j == n - 1)
@@ -356,8 +356,8 @@
     frames = at.shape[2]
     rows = CHAIN * frames
 
-    both = range(PAIR)
-    found = [band_at(meta, bands, pl.program_id(0) * PAIR + i) for i in both]
+    group = range(PAIR)
+    found = [band_at(meta, bands, pl.program_id(0) * PAIR + i) for i in group]
 
     @pl.when(pl.program_id(0) == 0)
     def _():
@@ -375,24 +375,24 @@
 
     pb = bias[pl.ds(BIAS_PROJ + 1, 1), :]
     normed = [
-        ln(at[:, i].reshape(rows, D) + (bo[:, i].reshape(rows, D).astype(F32) + pb)) for i in both
+        ln(at[:, i].reshape(rows, D) + (bo[:, i].reshape(rows, D).astype(F32) + pb)) for i in group
     ]
-    mg = [gain[pl.ds(GAIN_MASK + found[i][0], 1), :] for i in both]
-    mi = [(normed[i][0] * mg[i]).astype(BF) for i in both]
-    act_f = [jnp.tanh(mm(mi[i], um[i]) + wide_row(bias, BIAS_UP + 4 * found[i][0], 4)) for i in both]
+    mg = [gain[pl.ds(GAIN_MASK + found[i][0], 1), :] for i in group]
+    mi = [(normed[i][0] * mg[i]).astype(BF) for i in group]
+    act_f = [jnp.tanh(mm(mi[i], um[i]) + wide_row(bias, BIAS_UP + 4 * found[i][0], 4)) for i in group]
     act = [v.astype(BF) for v in act_f]
-    pre = [mm(act[i], dm[i]) + wide_row(bias, BIAS_DOWN + 2 * found[i][0], 2) for i in both]
+    pre = [mm(act[i], dm[i]) + wide_row(bias, BIAS_DOWN + 2 * found[i][0], 2) for i in group]
     og = []
-    for i in both:
+    for i in group:
         value = pre[i][:, :SUBF]
         gate = 0.5 * jnp.tanh(0.5 * pre[i][:, SUBF:]) + 0.5
         mask[:, i] = (value * gate).astype(BF).reshape(CHAIN, frames, SUBF)
         cg = cot[:, i].reshape(rows, D).astype(F32) * found[i][1].astype(F32) * gate
         og.append(jnp.concatenate([cg.astype(BF), (cg * value * (1.0 - gate)).astype(BF)], axis=-1))
-    pg = [(mm_nt(og[i], dm[i]) * (1.0 - act_f[i] * act_f[i])).astype(BF) for i in both]
-    dy = [mm_nt(pg[i], um[i]) for i in both]
+    pg = [(mm_nt(og[i], dm[i]) * (1.0 - act_f[i] * act_f[i])).astype(BF) for i in group]
+    dy = [mm_nt(pg[i], um[i]) for i in group]
     low = []
-    for i in both:
+    for i in group:
         halves(i, mm_tn(act[i], og[i]), UP_PART)
         halves(i, mm_tn(mi[i], pg[i]), 0)
         grad = ln_back(*normed[i], mg[i], dy[i])
@@ -401,9 +401,9 @@
         abl[:, i] = low[i].reshape(CHAIN, frames, D)
     sums = [
         [rowsum(v) for v in (dy[i] * normed[i][0], low[i].astype(F32), pg[i].astype(F32), og[i].astype(F32))]
-        for i in both
+        for i in group
     ]
-    for i in both:
+    for i in group:
         dmg, dpb, dub, ddb = sums[i]
         band = found[i][0]
 
@@ -441,7 +441,7 @@
 
     backward_chunk(
         keep, xs, ol, w, p, (h0, hk0, cf0, h1, hk1, cf1), dw, dp, db,
-        wt, pt, da, sh, rg, ch_s, cc_s, steps, chunk, frames, 2,
+        wt, pt, da, sh, rg, ch_s, cc_s, steps, chunk, frames, 7,
     )
 
     @pl.when(j == n - 1)
@@ -492,7 +492,7 @@
 
     backward_chunk(
         keep, xs, ol, w, p, (h0, hk0, cf0, h1, hk1, cf1), dw, dp, db,
-        wt, pt, da, sh, rg, ch_s, cc_s, steps, chunk, ROWS_T, 16,
+        wt, pt, da, sh, rg, ch_s, cc_s, steps, chunk, ROWS_T, 32,
     )
 
     @pl.when(j == n - 1)

time: 508 us -> 500 us (0.984)
  Pallas kernels: 252 us -> 244 us
where the time goes in v1:
time: 500 us; the launch traced here: 495 us
  Pallas kernels  244 us (49%)
  starting transfers between devices  64.3 us (13%)
  waiting for transfers between devices  60.7 us (12%)
  blocking collectives  47.4 us (9%)
  between operations  33.2 us (7%)
  other arithmetic  25.2 us (5%)
  local copies, waits for them, and re-layouts  20.2 us (4%)
    pallas_call x1, Pallas kernels, time_backward(): pl.pallas_call(functools.partial(time_backward_kernel, steps, chunk), gri...  93.5 us
    pallas_call x1, Pallas kernels, time_forward(): pl.pallas_call(functools.partial(time_forward_kernel, steps, chunk, table...  63.3 us
    ppermute x14, waiting for transfers between devices, swap_bit(): lax.ppermute(v, 'rows', [(r, r ^ 1 << bit) for r in range(lax.axis_size('...  48.7 us
    all_to_all x3, blocking collectives, across(): lax.all_to_all(v, 'rows', axis, axis, axis_index_groups=groups, tiled=True)  47.4 us
    ppermute x14, starting transfers between devices, swap_bit(): lax.ppermute(v, 'rows', [(r, r ^ 1 << bit) for r in range(lax.axis_size('...  34.7 us
    pallas_call x1, Pallas kernels, band_backward(): pl.pallas_call(functools.partial(band_backward_kernel, steps, chunk, tabl...  34.5 us
    pallas_call x1, Pallas kernels, band_forward(): pl.pallas_call(functools.partial(band_forward_kernel, steps, chunk, table...  23.7 us
    all_to_all x5, starting transfers between devices, across(): lax.all_to_all(v, 'rows', axis, axis, axis_index_groups=groups, tiled=True)  18.5 us
  transfers between devices with their start and end apart: 35, of which 12 were waited for; matrix products, arithmetic and copies ran while one was open for 6% of the time, Pallas kernels for 38%

profile of v1, /device:TPU:0, one launch (start us, length us, event | category | flops | bytes accessed | tf_op | source)
XLA Modules:
  0.0 494.9 jit_solution(16972993367652073396)
XLA Ops:
  11.2 7.1 %collective-permute-start = (bf16[52,1024]{1,0:T(8,128)(2,1)S(1)}, bf16[52,1024]{1,0:T(8,128)(2,1)S(1)}, u32[]{:S(2)}, u32[]{:S(2)}) collective-permute-start(bf16[52,1024]{1,0:T(8,128)(2,1)S(1)} %get-tuple-element.277), channel_id=1, source_target_pairs={{0,8},{1,9},{2,10},{3,11},{4,12},{5,13},{6,14},{7,15},{8,0},{9,1},... | collective-permute-start | bytes 319496 | tf_op jit(solution)/shard_map/ppermute | solution.py:844
  26.9 5.8 %collective-permute-start.2 = (bf16[384,128]{1,0:T(8,128)(2,1)S(1)}, bf16[384,128]{1,0:T(8,128)(2,1)S(1)}, u32[]{:S(2)}, u32[]{:S(2)}) collective-permute-start(bf16[384,128]{1,0:T(8,128)(2,1)S(1)} %fusion.23), channel_id=1, source_target_pairs={{0,8},{1,9},{2,10},{3,11},{4,12},{5,13},{6,14},{7,15},{8,0},{9,1},... | collective-permute-start | bytes 294920 | tf_op jit(solution)/shard_map/ppermute | solution.py:844
  37.5 3.5 all-to-all-start
  60.5 7.5 %collective-permute-done.8 = bf16[2,2,56,1024]{3,2,1,0:T(8,128)(2,1)} collective-permute-done((bf16[2,2,56,1024]{3,2,1,0:T(8,128)(2,1)}, bf16[2,2,56,1024]{3,2,1,0:T(8,128)(2,1)}, u32[]{:S(2)}, u32[]{:S(2)}) %collective-permute-start.8) | collective-permute-done | bytes 458784 | tf_op jit(solution)/shard_map/ppermute | solution.py:844
  79.1 3.7 all-to-all-start.2
  87.6 63.3 %time_forward.1 = (f32[4,12,64,128]{3,2,1,0:T(8,128)}, f32[4,12,64,128]{3,2,1,0:T(8,128)}, bf16[4,12,64,128]{3,2,1,0:T(8,128)(2,1)}, bf16[4096,128]{1,0:T(8,128)...) custom-call(f32[512]{0:T(512)} %pad_maximum_fusion.8.keep, ...), custom_call_target="tpu_custom_call" | custom-call | flops 65999998976 | bytes 66000000 | tf_op jit(solution)/shard_map/time_forward/pallas_call | solution.py:662
  151.0 4.2 all-to-all-start.1
  155.9 9.8 %all-to-all-done.1.rows_in = bf16[4,12,64,128]{3,2,1,0:T(8,128)(2,1)S(1)} async-done(((bf16[4,12,64,128]{3,2,1,0:T(8,128)(2,1)}), bf16[4,12,64,128]{3,2,1,0:T(8,128)(2,1)S(1)}, u32[]{:S(2)}, u32[]{:S(2)}) %all-to-all-start.1) | async-done | bytes 786464 | tf_op jit(solution)/shard_map/all_to_all | solution.py:815
  166.6 3.5 all-to-all-start.4
  170.6 23.7 %band_forward.1 = (bf16[4,12,64,128]{3,2,1,0:T(8,128)(2,1)}, bf16[2688,128]{1,0:T(8,128)(2,1)}, bf16[2,384,1024]{2,1,0:T(8,128)(2,1)}, bf16[42,64,256]{2,1,0:T(8...) custom-call(f32[84]{0:T(128)} %constant.125.clone.keep, ...), custom_call_target="tpu_custom_call" | custom-call | flops 27000000512 | bytes 27000000 | tf_op jit(solution)/shard_map/band_forward/pallas_call | solution.py:690
  194.3 15.1 %all_to_all.40.bo = bf16[4,12,64,128]{3,2,1,0:T(8,128)(2,1)} all-to-all(bf16[4,12,64,128]{3,2,1,0:T(8,128)(2,1)} %get-tuple-element.110), channel_id=1, replica_groups={{0,1,2,3},{4,5,6,7},{8,9,10,11},{12,13,14,15},{16,17,18,19},{20,21,22,2..., dimensions={0} | all-to-all | bytes 1572864 | tf_op jit(solution)/shard_map/all_to_all | solution.py:815
  209.4 11.0 %mask_stage.1 = (bf16[4,12,64,128]{3,2,1,0:T(8,128)(2,1)}, f32[4,12,64,128]{3,2,1,0:T(8,128)}, bf16[4,12,64,128]{3,2,1,0:T(8,128)(2,1)}, bf16[12,768,128]{2,1,0:...) custom-call(s32[48]{0:T(128)} %constant.124.clone.bands, s32[3]{0:T(128)} %pad_add_fusion.meta, ...), custom_call_target="tpu_custom_call" | custom-call | flops 16000000000 | bytes 16000000 | tf_op jit(solution)/shard_map/mask_stage/pallas_call | solution.py:716
  220.5 16.5 %all_to_all.41.ol_in = bf16[4,12,64,128]{3,2,1,0:T(8,128)(2,1)} all-to-all(bf16[4,12,64,128]{3,2,1,0:T(8,128)(2,1)} %get-tuple-element.112), channel_id=1, replica_groups={{0,1,2,3},{4,5,6,7},{8,9,10,11},{12,13,14,15},{16,17,18,19},{20,21,22,2..., dimensions={0} | all-to-all | bytes 1572864 | tf_op jit(solution)/shard_map/all_to_all | solution.py:815
  238.5 34.5 %band_backward.1 = (bf16[3072,128]{1,0:T(8,128)(2,1)}, bf16[3072,128]{1,0:T(8,128)(2,1)}, bf16[256,128]{1,0:T(8,128)(2,1)}, bf16[256,128]{1,0:T(8,128)(2,1)}, f3...) custom-call(f32[84]{0:T(128)} %constant.125.clone.keep, s32[3]{0:T(128)} %pad_add_fusion.meta, ...), custom_call_target="tpu_custom_call" | custom-call | flops 32000000000 | bytes 32000000 | tf_op jit(solution)/shard_map/band_backward/pallas_call | solution.py:765
  273.1 15.7 %all_to_all.42.bgrad = bf16[4,12,64,128]{3,2,1,0:T(8,128)(2,1)S(1)} all-to-all(bf16[4,12,64,128]{3,2,1,0:T(8,128)(2,1)} %get-tuple-element.123), channel_id=1, replica_groups={{0,1,2,3},{4,5,6,7},{8,9,10,11},{12,13,14,15},{16,17,18,19},{20,21,22,2..., dimensions={0} | all-to-all | bytes 1572864 | tf_op jit(solution)/shard_map/all_to_all | solution.py:815
  292.3 93.5 %time_backward.1 = (bf16[5536,128]{1,0:T(8,128)(2,1)}, bf16[5536,128]{1,0:T(8,128)(2,1)}, bf16[4,24,64,128]{3,2,1,0:T(8,128)(2,1)}) custom-call(f32[512]{0:T(512)} %pad_maximum_fusion.8.keep, s32[48]{0:T(128)} %constant.124.clone.bands, s32[3]{0:T(128)} %pad_add_fusion.meta, f32[1,1024]{1,0:T(1,128)} %constant.122.clone.scale, ...), custom_call_target="tpu_custom_call" | custom-call | flops 96000000000 | bytes 96000000 | tf_op jit(solution)/shard_map/time_backward/pallas_call | solution.py:787
  394.3 14.5 %collective-permute-done.16 = bf16[2208,128]{1,0:T(8,128)(2,1)S(1)} collective-permute-done((bf16[2208,128]{1,0:T(8,128)(2,1)}, bf16[2208,128]{1,0:T(8,128)(2,1)S(1)}, u32[]{:S(2)}, u32[]{:S(2)}) %collective-permute-start.16) | collective-permute-done | bytes 565280 | tf_op jit(solution)/shard_map/ppermute | solution.py:844
  410.0 8.5 %collective-permute-done.17 = bf16[1312,128]{1,0:T(8,128)(2,1)S(1)} collective-permute-done((bf16[1312,128]{1,0:T(8,128)(2,1)S(1)}, bf16[1312,128]{1,0:T(8,128)(2,1)S(1)}, u32[]{:S(2)}, u32[]{:S(2)}) %collective-permute-start.17) | collective-permute-done | bytes 335904 | tf_op jit(solution)/shard_map/ppermute | solution.py:844
  422.2 3.6 all-to-all-start.7
  425.8 7.4 %collective-permute-done.18 = bf16[2016,128]{1,0:T(8,128)(2,1)} collective-permute-done((bf16[2016,128]{1,0:T(8,128)(2,1)}, bf16[2016,128]{1,0:T(8,128)(2,1)}, u32[]{:S(2)}, u32[]{:S(2)}) %collective-permute-start.18) | collective-permute-done | bytes 516128 | tf_op jit(solution)/shard_map/ppermute | solution.py:844
  444.9 6.0 %collective-permute-done.19 = bf16[1216,128]{1,0:T(8,128)(2,1)S(1)} collective-permute-done((bf16[1216,128]{1,0:T(8,128)(2,1)S(1)}, bf16[1216,128]{1,0:T(8,128)(2,1)S(1)}, u32[]{:S(2)}, u32[]{:S(2)}) %collective-permute-start.19) | collective-permute-done | bytes 311328 | tf_op jit(solution)/shard_map/ppermute | solution.py:844
  456.2 3.3 totals.1
  472.5 4.9 collective-permute-start.25
  479.5 8.6 %finish.1 = (f32[1,1]{1,0:T(1,128)}, f32[328,128]{1,0:T(8,128)}, f32[328,128]{1,0:T(8,128)}, f32[328,128]{1,0:T(8,128)}, f32[328,128]{1,0:T(8,128)}, /*index=5*/...) custom-call(f32[8,128]{1,0:T(8,128)} %add.160.refs_0_, ...), custom_call_target="tpu_custom_call" | custom-call | flops 8000000000 | bytes 8000000 | tf_op jit(solution)/shard_map/finish/pallas_call | solution.py:1130
  (204 shorter events, 86.5 us)
Async XLA Ops:
  8.1 17.9 %collective-permute-start.1 = (bf16[128,128]{1,0:T(8,128)(2,1)S(1)}, bf16[128,128]{1,0:T(8,128)(2,1)S(1)}, u32[]{:S(2)}, u32[]{:S(2)}) collective-permute-start(bf16[128,128]{1,0:T(8,128)(2,1)S(1)} %slice.247), channel_id=1, source_target_pairs={{1,0},{2,1},{3,2},{4,3},{5,4},{6,5},{7,6},{8,7},{9,8},{10,9},{11,1... | collective-permute-start | bytes 98312 | tf_op jit(solution)/shard_map/ppermute | solution.py:877
  11.2 22.8 %collective-permute-start = (bf16[52,1024]{1,0:T(8,128)(2,1)S(1)}, bf16[52,1024]{1,0:T(8,128)(2,1)S(1)}, u32[]{:S(2)}, u32[]{:S(2)}) collective-permute-start(bf16[52,1024]{1,0:T(8,128)(2,1)S(1)} %get-tuple-element.277), channel_id=1, source_target_pairs={{0,8},{1,9},{2,10},{3,11},{4,12},{5,13},{6,14},{7,15},{8,0},{9,1},... | collective-permute-start | bytes 319496 | tf_op jit(solution)/shard_map/ppermute | solution.py:844
  20.4 26.5 %collective-permute-start.4 = (bf16[512,256]{1,0:T(8,128)(2,1)}, bf16[512,256]{1,0:T(8,128)(2,1)}, u32[]{:S(2)}, u32[]{:S(2)}) collective-permute-start(bf16[512,256]{1,0:T(8,128)(2,1)} %slice.248), channel_id=1, source_target_pairs={{1,0},{2,1},{3,2},{4,3},{5,4},{6,5},{7,6},{8,7},{9,8},{10,9},{11,1... | collective-permute-start | bytes 786440 | tf_op jit(solution)/shard_map/ppermute | solution.py:877
  21.8 23.3 %collective-permute-start.5 = (bf16[128,512]{1,0:T(8,128)(2,1)S(1)}, bf16[128,512]{1,0:T(8,128)(2,1)S(1)}, u32[]{:S(2)}, u32[]{:S(2)}) collective-permute-start(bf16[128,512]{1,0:T(8,128)(2,1)S(1)} %slice.250), channel_id=1, source_target_pairs={{1,0},{2,1},{3,2},{4,3},{5,4},{6,5},{7,6},{8,7},{9,8},{10,9},{11,1... | collective-permute-start | bytes 393224 | tf_op jit(solution)/shard_map/ppermute | solution.py:877
  26.9 14.3 %collective-permute-start.2 = (bf16[384,128]{1,0:T(8,128)(2,1)S(1)}, bf16[384,128]{1,0:T(8,128)(2,1)S(1)}, u32[]{:S(2)}, u32[]{:S(2)}) collective-permute-start(bf16[384,128]{1,0:T(8,128)(2,1)S(1)} %fusion.23), channel_id=1, source_target_pairs={{0,8},{1,9},{2,10},{3,11},{4,12},{5,13},{6,14},{7,15},{8,0},{9,1},... | collective-permute-start | bytes 294920 | tf_op jit(solution)/shard_map/ppermute | solution.py:844
  34.7 14.7 %collective-permute-start.6 = (bf16[2,52,1024]{2,1,0:T(8,128)(2,1)}, bf16[2,52,1024]{2,1,0:T(8,128)(2,1)}, u32[]{:S(2)}, u32[]{:S(2)}) collective-permute-start(bf16[2,52,1024]{2,1,0:T(8,128)(2,1)} %get-tuple-element.247), channel_id=1, source_target_pairs={{0,4},{1,5},{2,6},{3,7},{4,0},{5,1},{6,2},{7,3},{8,12},{9,13},{10,... | collective-permute-start | bytes 638984 | tf_op jit(solution)/shard_map/ppermute | solution.py:844
  37.5 17.7 %all-to-all-start = ((bf16[4,13,64,128]{3,2,1,0:T(8,128)(2,1)}), bf16[4,13,64,128]{3,2,1,0:T(8,128)(2,1)S(1)}, u32[]{:S(2)}, u32[]{:S(2)}) async-start(bf16[4,13,64,128]{3,2,1,0:T(8,128)(2,1)} %maximum_select_fusion.1), calls=%async_computation | async-start | bytes 1703936 | tf_op jit(solution)/shard_map/all_to_all | solution.py:815
  41.0 168.4 %all-gather.3.cloned.1.call-start = ((), (), s32[]{:S(2)}) async-start(), calls=%async_computation.10 | async-start | bytes 1966080 | tf_op jit(solution)/shard_map/all_gather | solution.py:947
  41.7 11.6 %collective-permute-start.3 = (bf16[2,384,128]{2,1,0:T(8,128)(2,1)S(1)}, bf16[2,384,128]{2,1,0:T(8,128)(2,1)S(1)}, u32[]{:S(2)}, u32[]{:S(2)}) collective-permute-start(bf16[2,384,128]{2,1,0:T(8,128)(2,1)S(1)} %maximum_select_fusion.12), channel_id=1, source_target_pairs={{0,4},{1,5},{2,6},{3,7},{4,0},{5,1},{6,2},{7,3},{8,12},{9,13},{10,... | collective-permute-start | bytes 589832 | tf_op jit(solution)/shard_map/ppermute | solution.py:844
  58.5 9.6 %collective-permute-start.8 = (bf16[2,2,56,1024]{3,2,1,0:T(8,128)(2,1)}, bf16[2,2,56,1024]{3,2,1,0:T(8,128)(2,1)}, u32[]{:S(2)}, u32[]{:S(2)}) collective-permute-start(bf16[2,2,56,1024]{3,2,1,0:T(8,128)(2,1)} %fusion.10), channel_id=1, source_target_pairs={{0,2},{1,3},{2,0},{3,1},{4,6},{5,7},{6,4},{7,5},{8,10},{9,11},{10,... | collective-permute-start | bytes 1376264 | tf_op jit(solution)/shard_map/ppermute | solution.py:844
  79.1 71.9 %all-to-all-start.2 = ((bf16[4,2,2,48,1024]{4,3,2,1,0:T(8,128)(2,1)}), bf16[4,2,2,48,1024]{4,3,2,1,0:T(8,128)(2,1)S(1)}, u32[]{:S(2)}, u32[]{:S(2)}) async-start(bf16[4,2,2,48,1024]{4,3,2,1,0:T(8,128)(2,1)} %broadcast_in_dim.47), calls=%async_computation.2 | async-start | bytes 3145728 | tf_op jit(solution)/shard_map/all_to_all | solution.py:815
  82.8 126.7 %all-gather.5.cloned.1.call-start = ((), (), s32[]{:S(2)}) async-start(), calls=%async_computation.11 | async-start | bytes 3932160 | tf_op jit(solution)/shard_map/all_gather | solution.py:947
  151.0 14.8 %all-to-all-start.1 = ((bf16[4,12,64,128]{3,2,1,0:T(8,128)(2,1)}), bf16[4,12,64,128]{3,2,1,0:T(8,128)(2,1)S(1)}, u32[]{:S(2)}, u32[]{:S(2)}) async-start(bf16[4,12,64,128]{3,2,1,0:T(8,128)(2,1)} %get-tuple-element.109), calls=%async_computation.1 | async-start | bytes 1572864 | tf_op jit(solution)/shard_map/all_to_all | solution.py:815
  166.6 27.6 %all-to-all-start.4 = ((bf16[4,12,64,128]{3,2,1,0:T(8,128)(2,1)}), bf16[4,12,64,128]{3,2,1,0:T(8,128)(2,1)S(1)}, u32[]{:S(2)}, u32[]{:S(2)}) async-start(bf16[4,12,64,128]{3,2,1,0:T(8,128)(2,1)} %get-tuple-element.111), calls=%async_computation.4 | async-start | bytes 1572864 | tf_op jit(solution)/shard_map/all_to_all | solution.py:815
  170.1 215.7 %reduce-scatter.5.cloned.1.call-start = ((), (), s32[]{:S(2)}) async-start(), calls=%async_computation.13 | async-start | bytes 983040 | tf_op jit(solution)/shard_map/reduce_scatter | solution.py:1225
  220.4 16.6 %collective-permute-start.11 = (bf16[12,768,128]{2,1,0:T(8,128)(2,1)}, bf16[12,768,128]{2,1,0:T(8,128)(2,1)S(1)}, u32[]{:S(2)}, u32[]{:S(2)}) collective-permute-start(bf16[12,768,128]{2,1,0:T(8,128)(2,1)} %get-tuple-element.116), channel_id=1, source_target_pairs={{0,16},{16,0},{1,17},{17,1},{2,18},{18,2},{3,19},{19,3},{4,20},{20... | collective-permute-start | bytes 7077896 | tf_op jit(solution)/shard_map/ppermute | solution.py:823
  273.0 17.7 %collective-permute-start.14 = (bf16[3072,128]{1,0:T(8,128)(2,1)}, bf16[3072,128]{1,0:T(8,128)(2,1)S(1)}, u32[]{:S(2)}, u32[]{:S(2)}) collective-permute-start(bf16[3072,128]{1,0:T(8,128)(2,1)} %get-tuple-element.147), channel_id=1, source_target_pairs={{0,16},{16,0},{1,17},{17,1},{2,18},{18,2},{3,19},{19,3},{4,20},{20... | collective-permute-start | bytes 2359304 | tf_op jit(solution)/shard_map/ppermute | solution.py:823
  291.7 96.7 %reduce-scatter.3.cloned.1.call-start = ((), (), s32[]{:S(2)}) async-start(), calls=%async_computation.12 | async-start | bytes 2949120 | tf_op jit(solution)/shard_map/reduce_scatter | solution.py:956
  393.4 15.4 %collective-permute-start.16 = (bf16[2208,128]{1,0:T(8,128)(2,1)}, bf16[2208,128]{1,0:T(8,128)(2,1)S(1)}, u32[]{:S(2)}, u32[]{:S(2)}) collective-permute-start(bf16[2208,128]{1,0:T(8,128)(2,1)} %pad_maximum_fusion), channel_id=1, source_target_pairs={{0,1},{1,0},{2,3},{3,2},{4,5},{5,4},{6,7},{7,6},{8,9},{9,8},{10,11... | collective-permute-start | bytes 1695752 | tf_op jit(solution)/shard_map/ppermute | solution.py:844
  420.4 12.8 %collective-permute-start.18 = (bf16[2016,128]{1,0:T(8,128)(2,1)}, bf16[2016,128]{1,0:T(8,128)(2,1)}, u32[]{:S(2)}, u32[]{:S(2)}) collective-permute-start(bf16[2016,128]{1,0:T(8,128)(2,1)} %pad_maximum_fusion.1), channel_id=1, source_target_pairs={{0,4},{1,5},{2,6},{3,7},{4,0},{5,1},{6,2},{7,3},{8,12},{9,13},{10,... | collective-permute-start | bytes 1548296 | tf_op jit(solution)/shard_map/ppermute | solution.py:844
  422.2 31.8 %all-to-all-start.7 = ((bf16[4,24,64,128]{3,2,1,0:T(8,128)(2,1)}), bf16[4,24,64,128]{3,2,1,0:T(8,128)(2,1)S(1)}, u32[]{:S(2)}, u32[]{:S(2)}) async-start(bf16[4,24,64,128]{3,2,1,0:T(8,128)(2,1)} %get-tuple-element.139), calls=%async_computation.7 | async-start | bytes 3145728 | tf_op jit(solution)/shard_map/all_to_all | solution.py:815
  425.8 13.2 %collective-permute-start.12 = (bf16[3,768,128]{2,1,0:T(8,128)(2,1)}, bf16[3,768,128]{2,1,0:T(8,128)(2,1)}, u32[]{:S(2)}, u32[]{:S(2)}) collective-permute-start(bf16[3,768,128]{2,1,0:T(8,128)(2,1)} %reduce-scatter.3.cloned.1.call-done.own), channel_id=1, source_target_pairs={{0,16},{16,0},{1,17},{17,1},{2,18},{18,2},{3,19},{19,3},{4,20},{20... | collective-permute-start | bytes 1769480 | tf_op jit(solution)/shard_map/ppermute | solution.py:823
  436.2 14.8 %collective-permute-start.19 = (bf16[1216,128]{1,0:T(8,128)(2,1)S(1)}, bf16[1216,128]{1,0:T(8,128)(2,1)S(1)}, u32[]{:S(2)}, u32[]{:S(2)}) collective-permute-start(bf16[1216,128]{1,0:T(8,128)(2,1)S(1)} %pad_maximum_fusion.3), channel_id=1, source_target_pairs={{0,8},{1,9},{2,10},{3,11},{4,12},{5,13},{6,14},{7,15},{8,0},{9,1},... | collective-permute-start | bytes 933896 | tf_op jit(solution)/shard_map/ppermute | solution.py:844
  442.1 11.9 %collective-permute-start.13 = (bf16[1536,128]{1,0:T(8,128)(2,1)}, bf16[1536,128]{1,0:T(8,128)(2,1)S(1)}, u32[]{:S(2)}, u32[]{:S(2)}) collective-permute-start(bf16[1536,128]{1,0:T(8,128)(2,1)} %get-tuple-element.145), channel_id=1, source_target_pairs={{0,1},{1,2},{2,3},{3,4},{4,5},{5,6},{6,7},{7,8},{8,9},{9,10},{10,1... | collective-permute-start | bytes 1179656 | tf_op jit(solution)/shard_map/ppermute | solution.py:1244
  (29 other events, 181.1 us)
Sparse Core Ops, SparseCore 0:
  72.4 36.1 all-gather.2
  110.2 62.3 all-gather.4
  291.8 23.9 reduce-scatter.4
  318.0 47.9 reduce-scatter.2
